TPU v7x, 128 devices: a whole 4x4x4 slice. The times are simulated.
128 devices in a mesh: flow: 2 (over x_lo), gy: 64 (over z, x_hi, y, core).
Axes of the slice: x: 4 (x_hi: 2, x_lo: 2; x = x_hi * 2 + x_lo), y: 4, z: 4, core: 2. Of those that a mesh axis runs over, the one named last changes fastest.
Arguments:
- initial_state: float32 [32, 16, 32768], P('flow', None, 'gy'), may hold values from -6 to 6
- sources: float32 [32, 16, 32768], P('flow', None, 'gy'), may hold values from -6 to 6
- inverse: float32 [32, 16, 16, 32768], P('flow', None, None, 'gy'), may hold values from -0.0084 to 0.168
- couplings: float32 [3, 16, 16], replicated, may hold values from 0 to 3
Outputs:
- relaxed_state: float32 [32, 16, 32768], P('flow', None, 'gy')
All inputs are finite; a program needn't handle non-finite values.
Results may differ from a plain program's by a relative error of at most 0.00018.
Values sent between devices are 32-bit elements; how exact they have to be, the bound alone decides.
No kernel may reach another device: no remote copies, remote signals or barrier semaphores. Data moves between devices by JAX's collectives and lax.ppermute only.
A program may use at most 192 MiB of HBM per device.

v0:
```python
import jax
import jax.numpy as jnp
from jax import lax
from jax.sharding import PartitionSpec as P

BX = 16
JAC = 4
CZ = 32


def with_halo(block, sides, width):
    for axis, dim in sides:
        count = lax.axis_size(axis)
        forward = [(i, i + 1) for i in range(count - 1)]
        backward = [(target, source) for source, target in forward]
        low = lax.ppermute(
            lax.slice_in_dim(block, block.shape[dim] - width, None, axis=dim), axis, forward
        )
        high = lax.ppermute(lax.slice_in_dim(block, 0, width, axis=dim), axis, backward)
        block = jnp.concatenate([low, block, high], axis=dim)
    return block


def shifted(block, axis, distance):
    devices = range(lax.axis_size(axis))
    route = [(i - distance, i) for i in devices if i - distance in devices]
    return lax.ppermute(block, axis, route)


def apply_coupling(matrix, values):
    return jnp.einsum("ts,psl->ptl", matrix, values, precision=lax.Precision.HIGHEST)


def z_neighbours(values):
    extent = values.shape[-1]
    z_position = lax.broadcasted_iota(jnp.int32, (extent,), 0) % CZ
    padded = jnp.pad(values, ((0, 0), (0, 0), (1, 1)))
    below_cells = jnp.where(z_position != 0, padded[..., :extent], jnp.zeros_like(values))
    above_cells = jnp.where(z_position != CZ - 1, padded[..., 2:], jnp.zeros_like(values))
    return below_cells + above_cells


def jacobi_step(values, y_padded, lower_plane, upper_plane, source_block, inverse_block, couplings):
    extent = values.shape[-1]
    stacked = jnp.concatenate([lower_plane[None], values, upper_plane[None]], 0)
    x_total = stacked[:-2] + stacked[2:]
    y_total = y_padded[..., :extent] + y_padded[..., 2 * CZ :]
    coupled = source_block + apply_coupling(couplings[0], x_total)
    coupled = coupled + apply_coupling(couplings[1], y_total)
    coupled = coupled + apply_coupling(couplings[2], z_neighbours(values))
    return jnp.sum(inverse_block * coupled[:, None], axis=2)


def shards(initial_state, sources, inverse, couplings):
    planes, species, cell_count = initial_state.shape
    row_count = cell_count // CZ
    block_count = planes // BX
    flow_count = lax.axis_size("flow")
    zero_plane = jnp.zeros((species, cell_count), jnp.float32)

    def relax(current_field, block_id, lower_plane, upper_plane):
        first_plane = block_id * BX
        values = current_field
        for step_id in range(JAC):
            y_padded = with_halo(
                values.reshape(BX, species, row_count, CZ), (("gy", 2),), 1
            ).reshape(BX, species, cell_count + 2 * CZ)
            values = jacobi_step(
                values, y_padded, lower_plane, upper_plane, sources, inverse, couplings
            )
        return current_field.at[first_plane : first_plane + BX].set(values)

    old_next = shifted(initial_state[0], "flow", -1)
    inflow = zero_plane
    forward = initial_state
    for round_id in range(flow_count):
        forward_current_field = initial_state
        forward_lower_plane = inflow
        forward_current_field = relax(forward_current_field, 0, forward_lower_plane, old_next)
        forward = forward_current_field
        inflow = shifted(forward[-1], "flow", 1)
    outflow = zero_plane
    relaxed = forward
    for round_id in range(flow_count):
        backward_current_field = forward
        for backward_block_id in reversed(range(block_count)):
            backward_current_field = relax(
                backward_current_field, backward_block_id, inflow, outflow
            )
        relaxed = backward_current_field
        if round_id + 1 < flow_count:
            outflow = shifted(relaxed[0], "flow", -1)
    return relaxed


def solution(mesh):
    return jax.shard_map(
        shards,
        mesh=mesh,
        in_specs=(P("flow", None, "gy"), P("flow", None, "gy"), P("flow", None, None, "gy"), P()),
        out_specs=P("flow", None, "gy"),
        check_vma=False,
    )
```

profile of v0, /device:TPU:29, one launch (start us, length us, event | category | flops | bytes accessed | tf_op | source)
XLA Modules:
  0.0 395.0 jit_solution(8428560847456123476)
XLA Ops:
  11.3 7.2 %collective-permute-done.2 = f32[16,16,1,32]{3,2,1,0:T(1,128)S(1)} collective-permute-done((f32[16,16,1,32]{3,2,1,0:T(1,128)S(1)}, f32[16,16,1,32]{3,2,1,0:T(1,128)S(1)}, u32[]{:S(2)}, u32[]{:S(2)}) %collective-permute-start.2) | collective-permute-done | bytes 32800 | tf_op jit(solution)/shard_map/ppermute | solution.py:19
  24.6 6.5 %multiply_reduce_fusion.15 = f32[16,16,512]{2,1,0:T(8,128)} fusion(f32[16,16,16,512]{3,2,1,0:T(8,128)} %param.22, f32[16,16,512]{2,1,0:T(8,128)S(1)} %fusion.2), kind=kLoop, calls=%fused_computation.15 | loop fusion | flops 4063232 | bytes 9437184 | tf_op jit(solution)/shard_map/reduce_sum | solution.py:51
  51.6 6.5 %multiply_reduce_fusion.14 = f32[16,16,512]{2,1,0:T(8,128)} fusion(f32[16,16,16,512]{3,2,1,0:T(8,128)} %param.22, f32[16,16,512]{2,1,0:T(8,128)S(1)} %fusion.5), kind=kLoop, calls=%fused_computation.14 | loop fusion | flops 4063232 | bytes 9437184 | tf_op jit(solution)/shard_map/reduce_sum | solution.py:51
  67.4 5.7 %collective-permute-done.6 = f32[16,16,1,32]{3,2,1,0:T(1,128)S(1)} collective-permute-done((f32[16,16,1,32]{3,2,1,0:T(1,128)S(1)}, f32[16,16,1,32]{3,2,1,0:T(1,128)S(1)}, u32[]{:S(2)}, u32[]{:S(2)}) %collective-permute-start.6) | collective-permute-done | bytes 32800 | tf_op jit(solution)/shard_map/ppermute | solution.py:19
  79.2 6.5 %multiply_reduce_fusion.13 = f32[16,16,512]{2,1,0:T(8,128)} fusion(f32[16,16,16,512]{3,2,1,0:T(8,128)} %param.22, f32[16,16,512]{2,1,0:T(8,128)S(1)} %fusion.8), kind=kLoop, calls=%fused_computation.13 | loop fusion | flops 4063232 | bytes 9437184 | tf_op jit(solution)/shard_map/reduce_sum | solution.py:51
  106.8 5.8 %multiply_reduce_fusion.12 = f32[16,16,512]{2,1,0:T(8,128)S(1)} fusion(f32[16,16,16,512]{3,2,1,0:T(8,128)} %param.22, f32[16,16,512]{2,1,0:T(8,128)S(1)} %fusion.11), kind=kLoop, calls=%fused_computation.12 | loop fusion | flops 4063232 | bytes 9437184 | tf_op jit(solution)/shard_map/reduce_sum | solution.py:51
  129.0 7.1 %collective-permute-done.11 = f32[16,16,1,32]{3,2,1,0:T(1,128)S(1)} collective-permute-done((f32[16,16,1,32]{3,2,1,0:T(1,128)S(1)}, f32[16,16,1,32]{3,2,1,0:T(1,128)S(1)}, u32[]{:S(2)}, u32[]{:S(2)}) %collective-permute-start.11) | collective-permute-done | bytes 32800 | tf_op jit(solution)/shard_map/ppermute | solution.py:19
  142.0 5.7 %multiply_reduce_fusion.10 = f32[16,16,512]{2,1,0:T(8,128)S(1)} fusion(f32[16,16,16,512]{3,2,1,0:T(8,128)} %param.22, f32[16,16,512]{2,1,0:T(8,128)S(1)} %fusion.17), kind=kLoop, calls=%fused_computation.10 | loop fusion | flops 4063232 | bytes 9437184 | tf_op jit(solution)/shard_map/reduce_sum | solution.py:51
  154.6 6.5 %collective-permute-done.13 = f32[16,16,1,32]{3,2,1,0:T(1,128)S(1)} collective-permute-done((f32[16,16,1,32]{3,2,1,0:T(1,128)S(1)}, f32[16,16,1,32]{3,2,1,0:T(1,128)S(1)}, u32[]{:S(2)}, u32[]{:S(2)}) %collective-permute-start.13) | collective-permute-done | bytes 32800 | tf_op jit(solution)/shard_map/ppermute | solution.py:19
  167.2 5.7 %multiply_reduce_fusion.9 = f32[16,16,512]{2,1,0:T(8,128)S(1)} fusion(f32[16,16,16,512]{3,2,1,0:T(8,128)} %param.22, f32[16,16,512]{2,1,0:T(8,128)S(1)} %fusion.20), kind=kLoop, calls=%fused_computation.9 | loop fusion | flops 4063232 | bytes 9437184 | tf_op jit(solution)/shard_map/reduce_sum | solution.py:51
  179.8 6.5 %collective-permute-done.15 = f32[16,16,1,32]{3,2,1,0:T(1,128)S(1)} collective-permute-done((f32[16,16,1,32]{3,2,1,0:T(1,128)S(1)}, f32[16,16,1,32]{3,2,1,0:T(1,128)S(1)}, u32[]{:S(2)}, u32[]{:S(2)}) %collective-permute-start.15) | collective-permute-done | bytes 32800 | tf_op jit(solution)/shard_map/ppermute | solution.py:19
  192.3 5.7 %multiply_reduce_fusion.8 = f32[16,16,512]{2,1,0:T(8,128)S(1)} fusion(f32[16,16,16,512]{3,2,1,0:T(8,128)} %param.22, f32[16,16,512]{2,1,0:T(8,128)S(1)} %fusion.23), kind=kLoop, calls=%fused_computation.8 | loop fusion | flops 4063232 | bytes 9437184 | tf_op jit(solution)/shard_map/reduce_sum | solution.py:51
  219.1 6.5 %multiply_reduce_fusion.7 = f32[16,16,512]{2,1,0:T(8,128)} fusion(f32[16,16,16,512]{3,2,1,0:T(8,128)} %param.22, f32[16,16,512]{2,1,0:T(8,128)S(1)} %fusion.26), kind=kLoop, calls=%fused_computation.7 | loop fusion | flops 4063232 | bytes 9437184 | tf_op jit(solution)/shard_map/reduce_sum | solution.py:51
  248.2 6.5 %multiply_reduce_fusion.6 = f32[16,16,512]{2,1,0:T(8,128)} fusion(f32[16,16,16,512]{3,2,1,0:T(8,128)} %param.22, f32[16,16,512]{2,1,0:T(8,128)S(1)} %fusion.29), kind=kLoop, calls=%fused_computation.6 | loop fusion | flops 4063232 | bytes 9437184 | tf_op jit(solution)/shard_map/reduce_sum | solution.py:51
  264.1 5.8 %collective-permute-done.22 = f32[16,16,1,32]{3,2,1,0:T(1,128)S(1)} collective-permute-done((f32[16,16,1,32]{3,2,1,0:T(1,128)S(1)}, f32[16,16,1,32]{3,2,1,0:T(1,128)S(1)}, u32[]{:S(2)}, u32[]{:S(2)}) %collective-permute-start.22) | collective-permute-done | bytes 32800 | tf_op jit(solution)/shard_map/ppermute | solution.py:19
  276.0 6.5 %multiply_reduce_fusion.5 = f32[16,16,512]{2,1,0:T(8,128)} fusion(f32[16,16,16,512]{3,2,1,0:T(8,128)} %param.22, f32[16,16,512]{2,1,0:T(8,128)S(1)} %fusion.32), kind=kLoop, calls=%fused_computation.5 | loop fusion | flops 4063232 | bytes 9437184 | tf_op jit(solution)/shard_map/reduce_sum | solution.py:51
  291.7 5.7 %collective-permute-done.24 = f32[16,16,1,32]{3,2,1,0:T(1,128)S(1)} collective-permute-done((f32[16,16,1,32]{3,2,1,0:T(1,128)S(1)}, f32[16,16,1,32]{3,2,1,0:T(1,128)S(1)}, u32[]{:S(2)}, u32[]{:S(2)}) %collective-permute-start.24) | collective-permute-done | bytes 32800 | tf_op jit(solution)/shard_map/ppermute | solution.py:19
  303.5 5.8 %multiply_reduce_fusion.4 = f32[16,16,512]{2,1,0:T(8,128)S(1)} fusion(f32[16,16,16,512]{3,2,1,0:T(8,128)} %param.22, f32[16,16,512]{2,1,0:T(8,128)S(1)} %fusion.35), kind=kLoop, calls=%fused_computation.4 | loop fusion | flops 4063232 | bytes 9437184 | tf_op jit(solution)/shard_map/reduce_sum | solution.py:51
  325.1 7.0 %collective-permute-done.27 = f32[16,16,1,32]{3,2,1,0:T(1,128)S(1)} collective-permute-done((f32[16,16,1,32]{3,2,1,0:T(1,128)S(1)}, f32[16,16,1,32]{3,2,1,0:T(1,128)S(1)}, u32[]{:S(2)}, u32[]{:S(2)}) %collective-permute-start.27) | collective-permute-done | bytes 32800 | tf_op jit(solution)/shard_map/ppermute | solution.py:19
  338.1 5.7 %multiply_reduce_fusion.2 = f32[16,16,512]{2,1,0:T(8,128)S(1)} fusion(f32[16,16,16,512]{3,2,1,0:T(8,128)} %param.22, f32[16,16,512]{2,1,0:T(8,128)S(1)} %fusion.41), kind=kLoop, calls=%fused_computation.2 | loop fusion | flops 4063232 | bytes 9437184 | tf_op jit(solution)/shard_map/reduce_sum | solution.py:51
  350.8 6.5 %collective-permute-done.29 = f32[16,16,1,32]{3,2,1,0:T(1,128)S(1)} collective-permute-done((f32[16,16,1,32]{3,2,1,0:T(1,128)S(1)}, f32[16,16,1,32]{3,2,1,0:T(1,128)S(1)}, u32[]{:S(2)}, u32[]{:S(2)}) %collective-permute-start.29) | collective-permute-done | bytes 32800 | tf_op jit(solution)/shard_map/ppermute | solution.py:19
  363.2 5.7 %multiply_reduce_fusion.1 = f32[16,16,512]{2,1,0:T(8,128)S(1)} fusion(f32[16,16,16,512]{3,2,1,0:T(8,128)} %param.22, f32[16,16,512]{2,1,0:T(8,128)S(1)} %fusion.44), kind=kLoop, calls=%fused_computation.1 | loop fusion | flops 4063232 | bytes 9437184 | tf_op jit(solution)/shard_map/reduce_sum | solution.py:51
  376.1 6.2 %collective-permute-done.31 = f32[16,16,1,32]{3,2,1,0:T(1,128)S(1)} collective-permute-done((f32[16,16,1,32]{3,2,1,0:T(1,128)S(1)}, f32[16,16,1,32]{3,2,1,0:T(1,128)S(1)}, u32[]{:S(2)}, u32[]{:S(2)}) %collective-permute-start.31) | collective-permute-done | bytes 32800 | tf_op jit(solution)/shard_map/ppermute | solution.py:19
  388.4 6.5 %multiply_reduce_fusion = f32[16,16,512]{2,1,0:T(8,128)} fusion(f32[16,16,16,512]{3,2,1,0:T(8,128)} %param.22, f32[16,16,512]{2,1,0:T(8,128)S(1)} %fusion.47), kind=kLoop, calls=%fused_computation | loop fusion | flops 4063232 | bytes 9437184 | tf_op jit(solution)/shard_map/reduce_sum | solution.py:51
  (229 shorter events, 243.9 us)
Async XLA Ops:
  0.8 22.9 %collective-permute-start = (f32[16,512]{1,0:T(8,128)S(1)}, f32[16,512]{1,0:T(8,128)S(1)}, u32[]{:S(2)}, u32[]{:S(2)}) collective-permute-start(f32[16,512]{1,0:T(8,128)S(1)} %slice_bitcast_fusion.3), channel_id=1, source_target_pairs={{64,0},{65,1},{66,2},{67,3},{68,4},{69,5},{70,6},{71,7},{72,8},{73... | collective-permute-start | bytes 98312 | tf_op jit(solution)/shard_map/ppermute | solution.py:27
  7.7 10.8 %collective-permute-start.2 = (f32[16,16,1,32]{3,2,1,0:T(1,128)S(1)}, f32[16,16,1,32]{3,2,1,0:T(1,128)S(1)}, u32[]{:S(2)}, u32[]{:S(2)}) collective-permute-start(f32[16,16,1,32]{3,2,1,0:T(1,128)S(1)} %get-tuple-element.112), channel_id=1, source_target_pairs={{1,0},{2,1},{3,2},{4,3},{5,4},{6,5},{7,6},{8,7},{9,8},{10,9},{11,1... | collective-permute-start | bytes 98312 | tf_op jit(solution)/shard_map/ppermute | solution.py:19
  32.9 7.4 %collective-permute-start.3 = (f32[16,16,1,32]{3,2,1,0:T(1,128)S(1)}, f32[16,16,1,32]{3,2,1,0:T(1,128)S(1)}, u32[]{:S(2)}, u32[]{:S(2)}) collective-permute-start(f32[16,16,1,32]{3,2,1,0:T(1,128)S(1)} %get-tuple-element.109), channel_id=1, source_target_pairs={{0,1},{1,2},{2,3},{3,4},{4,5},{5,6},{6,7},{7,8},{8,9},{9,10},{10,1... | collective-permute-start | bytes 98312 | tf_op jit(solution)/shard_map/ppermute | solution.py:16
  34.8 10.8 %collective-permute-start.4 = (f32[16,16,1,32]{3,2,1,0:T(1,128)S(1)}, f32[16,16,1,32]{3,2,1,0:T(1,128)S(1)}, u32[]{:S(2)}, u32[]{:S(2)}) collective-permute-start(f32[16,16,1,32]{3,2,1,0:T(1,128)S(1)} %get-tuple-element.110), channel_id=1, source_target_pairs={{1,0},{2,1},{3,2},{4,3},{5,4},{6,5},{7,6},{8,7},{9,8},{10,9},{11,1... | collective-permute-start | bytes 98312 | tf_op jit(solution)/shard_map/ppermute | solution.py:19
  59.9 7.5 %collective-permute-start.5 = (f32[16,16,1,32]{3,2,1,0:T(1,128)S(1)}, f32[16,16,1,32]{3,2,1,0:T(1,128)S(1)}, u32[]{:S(2)}, u32[]{:S(2)}) collective-permute-start(f32[16,16,1,32]{3,2,1,0:T(1,128)S(1)} %get-tuple-element.107), channel_id=1, source_target_pairs={{0,1},{1,2},{2,3},{3,4},{4,5},{5,6},{6,7},{7,8},{8,9},{9,10},{10,1... | collective-permute-start | bytes 98312 | tf_op jit(solution)/shard_map/ppermute | solution.py:16
  62.3 10.8 %collective-permute-start.6 = (f32[16,16,1,32]{3,2,1,0:T(1,128)S(1)}, f32[16,16,1,32]{3,2,1,0:T(1,128)S(1)}, u32[]{:S(2)}, u32[]{:S(2)}) collective-permute-start(f32[16,16,1,32]{3,2,1,0:T(1,128)S(1)} %get-tuple-element.108), channel_id=1, source_target_pairs={{1,0},{2,1},{3,2},{4,3},{5,4},{6,5},{7,6},{8,7},{9,8},{10,9},{11,1... | collective-permute-start | bytes 98312 | tf_op jit(solution)/shard_map/ppermute | solution.py:19
  87.5 7.7 %collective-permute-start.7 = (f32[16,16,1,32]{3,2,1,0:T(1,128)S(1)}, f32[16,16,1,32]{3,2,1,0:T(1,128)S(1)}, u32[]{:S(2)}, u32[]{:S(2)}) collective-permute-start(f32[16,16,1,32]{3,2,1,0:T(1,128)S(1)} %get-tuple-element.105), channel_id=1, source_target_pairs={{0,1},{1,2},{2,3},{3,4},{4,5},{5,6},{6,7},{7,8},{8,9},{9,10},{10,1... | collective-permute-start | bytes 98312 | tf_op jit(solution)/shard_map/ppermute | solution.py:16
  89.9 10.8 %collective-permute-start.8 = (f32[16,16,1,32]{3,2,1,0:T(1,128)S(1)}, f32[16,16,1,32]{3,2,1,0:T(1,128)S(1)}, u32[]{:S(2)}, u32[]{:S(2)}) collective-permute-start(f32[16,16,1,32]{3,2,1,0:T(1,128)S(1)} %get-tuple-element.106), channel_id=1, source_target_pairs={{1,0},{2,1},{3,2},{4,3},{5,4},{6,5},{7,6},{8,7},{9,8},{10,9},{11,1... | collective-permute-start | bytes 98312 | tf_op jit(solution)/shard_map/ppermute | solution.py:19
  125.2 10.8 %collective-permute-start.11 = (f32[16,16,1,32]{3,2,1,0:T(1,128)S(1)}, f32[16,16,1,32]{3,2,1,0:T(1,128)S(1)}, u32[]{:S(2)}, u32[]{:S(2)}) collective-permute-start(f32[16,16,1,32]{3,2,1,0:T(1,128)S(1)} %get-tuple-element.104), channel_id=1, source_target_pairs={{1,0},{2,1},{3,2},{4,3},{5,4},{6,5},{7,6},{8,7},{9,8},{10,9},{11,1... | collective-permute-start | bytes 98312 | tf_op jit(solution)/shard_map/ppermute | solution.py:19
  150.4 10.8 %collective-permute-start.13 = (f32[16,16,1,32]{3,2,1,0:T(1,128)S(1)}, f32[16,16,1,32]{3,2,1,0:T(1,128)S(1)}, u32[]{:S(2)}, u32[]{:S(2)}) collective-permute-start(f32[16,16,1,32]{3,2,1,0:T(1,128)S(1)} %get-tuple-element.102), channel_id=1, source_target_pairs={{1,0},{2,1},{3,2},{4,3},{5,4},{6,5},{7,6},{8,7},{9,8},{10,9},{11,1... | collective-permute-start | bytes 98312 | tf_op jit(solution)/shard_map/ppermute | solution.py:19
  175.5 10.8 %collective-permute-start.15 = (f32[16,16,1,32]{3,2,1,0:T(1,128)S(1)}, f32[16,16,1,32]{3,2,1,0:T(1,128)S(1)}, u32[]{:S(2)}, u32[]{:S(2)}) collective-permute-start(f32[16,16,1,32]{3,2,1,0:T(1,128)S(1)} %get-tuple-element.100), channel_id=1, source_target_pairs={{1,0},{2,1},{3,2},{4,3},{5,4},{6,5},{7,6},{8,7},{9,8},{10,9},{11,1... | collective-permute-start | bytes 98312 | tf_op jit(solution)/shard_map/ppermute | solution.py:19
  200.4 9.2 %collective-permute-start.17 = (f32[16,16,1,32]{3,2,1,0:T(1,128)S(1)}, f32[16,16,1,32]{3,2,1,0:T(1,128)S(1)}, u32[]{:S(2)}, u32[]{:S(2)}) collective-permute-start(f32[16,16,1,32]{3,2,1,0:T(1,128)S(1)} %get-tuple-element.97), channel_id=1, source_target_pairs={{0,1},{1,2},{2,3},{3,4},{4,5},{5,6},{6,7},{7,8},{8,9},{9,10},{10,1... | collective-permute-start | bytes 98312 | tf_op jit(solution)/shard_map/ppermute | solution.py:16
  202.3 10.8 %collective-permute-start.18 = (f32[16,16,1,32]{3,2,1,0:T(1,128)S(1)}, f32[16,16,1,32]{3,2,1,0:T(1,128)S(1)}, u32[]{:S(2)}, u32[]{:S(2)}) collective-permute-start(f32[16,16,1,32]{3,2,1,0:T(1,128)S(1)} %get-tuple-element.98), channel_id=1, source_target_pairs={{1,0},{2,1},{3,2},{4,3},{5,4},{6,5},{7,6},{8,7},{9,8},{10,9},{11,1... | collective-permute-start | bytes 98312 | tf_op jit(solution)/shard_map/ppermute | solution.py:19
  204.7 13.7 %collective-permute-start.16 = (f32[16,512]{1,0:T(8,128)S(1)}, f32[16,512]{1,0:T(8,128)S(1)}, u32[]{:S(2)}, u32[]{:S(2)}) collective-permute-start(f32[16,512]{1,0:T(8,128)S(1)} %slice_bitcast_fusion.1), channel_id=1, source_target_pairs={{0,64},{1,65},{2,66},{3,67},{4,68},{5,69},{6,70},{7,71},{8,72},{9,... | collective-permute-start | bytes 98312 | tf_op jit(solution)/shard_map/ppermute | solution.py:27
  227.5 9.1 %collective-permute-start.19 = (f32[16,16,1,32]{3,2,1,0:T(1,128)S(1)}, f32[16,16,1,32]{3,2,1,0:T(1,128)S(1)}, u32[]{:S(2)}, u32[]{:S(2)}) collective-permute-start(f32[16,16,1,32]{3,2,1,0:T(1,128)S(1)} %get-tuple-element.95), channel_id=1, source_target_pairs={{0,1},{1,2},{2,3},{3,4},{4,5},{5,6},{6,7},{7,8},{8,9},{9,10},{10,1... | collective-permute-start | bytes 98312 | tf_op jit(solution)/shard_map/ppermute | solution.py:16
  231.3 10.8 %collective-permute-start.20 = (f32[16,16,1,32]{3,2,1,0:T(1,128)S(1)}, f32[16,16,1,32]{3,2,1,0:T(1,128)S(1)}, u32[]{:S(2)}, u32[]{:S(2)}) collective-permute-start(f32[16,16,1,32]{3,2,1,0:T(1,128)S(1)} %get-tuple-element.96), channel_id=1, source_target_pairs={{1,0},{2,1},{3,2},{4,3},{5,4},{6,5},{7,6},{8,7},{9,8},{10,9},{11,1... | collective-permute-start | bytes 98312 | tf_op jit(solution)/shard_map/ppermute | solution.py:19
  256.5 7.6 %collective-permute-start.21 = (f32[16,16,1,32]{3,2,1,0:T(1,128)S(1)}, f32[16,16,1,32]{3,2,1,0:T(1,128)S(1)}, u32[]{:S(2)}, u32[]{:S(2)}) collective-permute-start(f32[16,16,1,32]{3,2,1,0:T(1,128)S(1)} %get-tuple-element.93), channel_id=1, source_target_pairs={{0,1},{1,2},{2,3},{3,4},{4,5},{5,6},{6,7},{7,8},{8,9},{9,10},{10,1... | collective-permute-start | bytes 98312 | tf_op jit(solution)/shard_map/ppermute | solution.py:16
  259.1 10.8 %collective-permute-start.22 = (f32[16,16,1,32]{3,2,1,0:T(1,128)S(1)}, f32[16,16,1,32]{3,2,1,0:T(1,128)S(1)}, u32[]{:S(2)}, u32[]{:S(2)}) collective-permute-start(f32[16,16,1,32]{3,2,1,0:T(1,128)S(1)} %get-tuple-element.94), channel_id=1, source_target_pairs={{1,0},{2,1},{3,2},{4,3},{5,4},{6,5},{7,6},{8,7},{9,8},{10,9},{11,1... | collective-permute-start | bytes 98312 | tf_op jit(solution)/shard_map/ppermute | solution.py:19
  284.3 7.4 %collective-permute-start.23 = (f32[16,16,1,32]{3,2,1,0:T(1,128)S(1)}, f32[16,16,1,32]{3,2,1,0:T(1,128)S(1)}, u32[]{:S(2)}, u32[]{:S(2)}) collective-permute-start(f32[16,16,1,32]{3,2,1,0:T(1,128)S(1)} %get-tuple-element.91), channel_id=1, source_target_pairs={{0,1},{1,2},{2,3},{3,4},{4,5},{5,6},{6,7},{7,8},{8,9},{9,10},{10,1... | collective-permute-start | bytes 98312 | tf_op jit(solution)/shard_map/ppermute | solution.py:16
  286.6 10.8 %collective-permute-start.24 = (f32[16,16,1,32]{3,2,1,0:T(1,128)S(1)}, f32[16,16,1,32]{3,2,1,0:T(1,128)S(1)}, u32[]{:S(2)}, u32[]{:S(2)}) collective-permute-start(f32[16,16,1,32]{3,2,1,0:T(1,128)S(1)} %get-tuple-element.92), channel_id=1, source_target_pairs={{1,0},{2,1},{3,2},{4,3},{5,4},{6,5},{7,6},{8,7},{9,8},{10,9},{11,1... | collective-permute-start | bytes 98312 | tf_op jit(solution)/shard_map/ppermute | solution.py:19
  317.8 7.3 %collective-permute-start.26 = (f32[16,16,1,32]{3,2,1,0:T(1,128)S(1)}, f32[16,16,1,32]{3,2,1,0:T(1,128)S(1)}, u32[]{:S(2)}, u32[]{:S(2)}) collective-permute-start(f32[16,16,1,32]{3,2,1,0:T(1,128)S(1)} %get-tuple-element.89), channel_id=1, source_target_pairs={{0,1},{1,2},{2,3},{3,4},{4,5},{5,6},{6,7},{7,8},{8,9},{9,10},{10,1... | collective-permute-start | bytes 98312 | tf_op jit(solution)/shard_map/ppermute | solution.py:16
  321.3 10.8 %collective-permute-start.27 = (f32[16,16,1,32]{3,2,1,0:T(1,128)S(1)}, f32[16,16,1,32]{3,2,1,0:T(1,128)S(1)}, u32[]{:S(2)}, u32[]{:S(2)}) collective-permute-start(f32[16,16,1,32]{3,2,1,0:T(1,128)S(1)} %get-tuple-element.90), channel_id=1, source_target_pairs={{1,0},{2,1},{3,2},{4,3},{5,4},{6,5},{7,6},{8,7},{9,8},{10,9},{11,1... | collective-permute-start | bytes 98312 | tf_op jit(solution)/shard_map/ppermute | solution.py:19
  346.4 10.8 %collective-permute-start.29 = (f32[16,16,1,32]{3,2,1,0:T(1,128)S(1)}, f32[16,16,1,32]{3,2,1,0:T(1,128)S(1)}, u32[]{:S(2)}, u32[]{:S(2)}) collective-permute-start(f32[16,16,1,32]{3,2,1,0:T(1,128)S(1)} %get-tuple-element.88), channel_id=1, source_target_pairs={{1,0},{2,1},{3,2},{4,3},{5,4},{6,5},{7,6},{8,7},{9,8},{10,9},{11,1... | collective-permute-start | bytes 98312 | tf_op jit(solution)/shard_map/ppermute | solution.py:19
  371.6 10.8 %collective-permute-start.31 = (f32[16,16,1,32]{3,2,1,0:T(1,128)S(1)}, f32[16,16,1,32]{3,2,1,0:T(1,128)S(1)}, u32[]{:S(2)}, u32[]{:S(2)}) collective-permute-start(f32[16,16,1,32]{3,2,1,0:T(1,128)S(1)} %get-tuple-element.86), channel_id=1, source_target_pairs={{1,0},{2,1},{3,2},{4,3},{5,4},{6,5},{7,6},{8,7},{9,8},{10,9},{11,1... | collective-permute-start | bytes 98312 | tf_op jit(solution)/shard_map/ppermute | solution.py:19
  (41 other events, 228.4 us)
where the time goes:
time: 403 us; the launch traced here: 395 us
  other arithmetic  122 us (30%)
  waiting for transfers between devices  88.5 us (22%)
  starting transfers between devices  81.1 us (20%)
  matrix products  51.1 us (13%)
  local copies, waits for them, and re-layouts  50.5 us (13%)
    reduce_sum x16, other arithmetic, jacobi_step(): return jnp.sum(inverse_block * coupled[:, None], axis=2)  89.8 us
    ppermute x14, waiting for transfers between devices, with_halo(): lax.ppermute(lax.slice_in_dim(block, 0, width, axis=dim), axis, backward)  84.1 us
    dot_general x44, matrix products, apply_coupling(): jnp.einsum('ts,psl->ptl', matrix, values, precision=lax.Precision.HIGHEST)  51.1 us
    ppermute x14, starting transfers between devices, with_halo(): lax.ppermute(lax.slice_in_dim(block, block.shape[dim] - width, None, axis...  35.3 us
    ppermute x14, starting transfers between devices, with_halo(): lax.ppermute(lax.slice_in_dim(block, 0, width, axis=dim), axis, backward)  33.6 us
    concatenate x14, other arithmetic, with_halo(): block = jnp.concatenate([low, block, high], axis=dim)  32.4 us
    reshape x14, local copies, waits for them, and re-layouts, relax(): y_padded = with_halo(values.reshape(BX, species, row_count, CZ), (('gy',...  31.7 us
    reshape x14, local copies, waits for them, and re-layouts, relax(): values.reshape(BX, species, row_count, CZ)  15.2 us
  transfers between devices with their start and end apart: 32, of which 16 were waited for; matrix products, arithmetic and copies ran while one was open for 10% of the time, Pallas kernels for 0%

commit v1 on v0

v1 whole, which is shorter than its diff:
```python
import functools

import jax
import jax.numpy as jnp
from jax import lax
from jax.experimental import pallas as pl
from jax.experimental.pallas import tpu as pltpu
from jax.sharding import PartitionSpec as P

S = 16
BX = 16
CZ = 32
OWN = 512
T = 128
F32 = jnp.float32
BF16 = jnp.bfloat16

INV_ROWS = 6 * 256
SV0 = INV_ROWS
PAY1 = INV_ROWS + 18 * S
PAY2 = 3 * 256


def slot_iota(rows):
    return lax.broadcasted_iota(jnp.int32, (rows, T), 1) // CZ


def plane_of(flow, d):
    return jnp.where(flow == 1, d, BX - 1 - d)


def split_couplings(c):
    hi = c.astype(BF16)
    lo = (c - hi.astype(F32)).astype(BF16)
    return jnp.concatenate([hi, hi, lo], axis=1)


def mm(cb, v):
    hi = v.astype(BF16)
    lo = (v - hi.astype(F32)).astype(BF16)
    return jnp.dot(cb, jnp.concatenate([hi, lo, hi], axis=0), preferred_element_type=F32)


def z_masks(width):
    z = lax.broadcasted_iota(jnp.int32, (S, width), 1) % CZ
    return z != 0, z != CZ - 1


def yz_terms(u1, u2, masks):
    width = u1.shape[1]
    below, above = masks
    y = pltpu.roll(u1, CZ, 1) + pltpu.roll(u1, width - CZ, 1)
    z = jnp.where(below, pltpu.roll(u2, 1, 1), 0.0) + jnp.where(above, pltpu.roll(u2, width - 1, 1), 0.0)
    return y + z


def apply_inverse(pieces):
    out = []
    for get, c in pieces:
        acc = get(0) * c[0:1, :]
        for s in range(1, S):
            acc = acc + get(s) * c[s : s + 1, :]
        out.append(acc)
    return out


def low_high(slots, right, left):
    return jnp.where(slots < 2, right, left)


def pack_kernel(info, state, src, inv, pa1, pb1, pa2, pb2, g, ga, gb, edge, sem):
    flow, odd = info[0], info[1]

    def copy(i):
        d, side = i // 2, i % 2
        return pltpu.make_async_copy(
            inv.at[plane_of(flow, d), :, pl.ds(side * 384, T)], edge.at[i], sem.at[i]
        )

    for i in range(2 * BX):
        copy(i).start()
    slots = slot_iota(S)
    g[...] = state[plane_of(flow, 0)]
    for out1, out2, right in ((pa1, pa2, 1 - odd), (pb1, pb2, odd)):
        lane0 = pl.multiple_of(right * 384, T)
        row = SV0
        for d in range(BX):
            p = plane_of(flow, d)
            v = state[p, :, pl.ds(lane0, T)]
            r = src[p, :, pl.ds(lane0, T)]
            if d < 2:
                out1[row : row + S] = v
                out1[row + S : row + 2 * S] = r
                row += 2 * S
            else:
                keep = (slots < 2) == (right == 0)
                out1[row : row + S] = jnp.where(keep, v, pltpu.roll(r, 64, 1))
                row += S
    for out, right in ((ga, 1 - odd), (gb, odd)):
        out[...] = state[plane_of(flow, 0), :, pl.ds(pl.multiple_of(right * 384, T), T)]
    for i in range(2 * BX):
        copy(i).wait()
    slots8 = slot_iota(8)
    for out1, out2, right in ((pa1, pa2, 1 - odd), (pb1, pb2, odd)):
        for d in range(2):
            out1[d * 256 : (d + 1) * 256] = edge[2 * d + right]
        near = jnp.where(right == 1, 3, 0)
        next_ = jnp.where(right == 1, 2, 1)
        mask1 = [slots8 == ((near + q) & 3) for q in range(4)]
        mask2 = [slots8 == ((next_ + q) & 3) for q in range(4)]

        def rows(i, _, right=right, out1=out1, out2=out2, mask1=mask1, mask2=mask2):
            at = pl.multiple_of(i * 8, 8)
            for grp in range(3):
                one = two = jnp.zeros((8, T), F32)
                for q in range(4):
                    x = edge[2 * (2 + 4 * grp + q) + right, pl.ds(at, 8), :]
                    x = pltpu.roll(x, CZ * q, 1) if q else x
                    one = jnp.where(mask1[q], x, one)
                    two = jnp.where(mask2[q], x, two)
                out1[pl.ds((2 + grp) * 256 + at, 8), :] = one
                out2[pl.ds(grp * 256 + at, 8), :] = two
            keep = (slots8 < 2) == (right == 0)
            a = edge[28 + right, pl.ds(at, 8), :]
            b = edge[30 + right, pl.ds(at, 8), :]
            out1[pl.ds(5 * 256 + at, 8), :] = jnp.where(keep, a, pltpu.roll(b, 64, 1))
            return 0

        lax.fori_loop(0, 32, rows, 0, unroll=4)


def pack(info, state, src, inv):
    f = jax.ShapeDtypeStruct
    vm = pl.BlockSpec(memory_space=pltpu.VMEM)
    return pl.pallas_call(
        pack_kernel,
        in_specs=[pl.BlockSpec(memory_space=pltpu.SMEM), vm, vm, pl.BlockSpec(memory_space=pl.ANY)],
        out_specs=[vm] * 7,
        out_shape=[f((PAY1, T), F32)] * 2 + [f((PAY2, T), F32)] * 2 + [f((S, OWN), F32)] + [f((S, T), F32)] * 2,
        scratch_shapes=[pltpu.VMEM((2 * BX, 256, T), F32), pltpu.SemaphoreType.DMA((2 * BX,))],
        compiler_params=pltpu.CompilerParams(vmem_limit_bytes=24 * 2**20),
        name="pack",
    )(info, state, src, inv)


def turn_kernel(info, inv, out, buf, sem):
    flow = info[0]

    def copy(i):
        d, tile = i // 4, i % 4
        return pltpu.make_async_copy(
            inv.at[plane_of(flow, d), :, pl.ds(tile * T, T)], buf.at[i], sem.at[d]
        )

    for i in range(4 * BX):
        copy(i).start()
    for d in range(BX):
        for tile in range(4):
            copy(4 * d + tile).wait()
        for tile in range(4):
            for s in range(S):
                out[d, s, :, tile * T : (tile + 1) * T] = buf[4 * d + tile, pl.ds(s, S, stride=S), :]


def turn(info, inv):
    return pl.pallas_call(
        turn_kernel,
        in_specs=[pl.BlockSpec(memory_space=pltpu.SMEM), pl.BlockSpec(memory_space=pl.ANY)],
        out_specs=pl.BlockSpec(memory_space=pltpu.VMEM),
        out_shape=jax.ShapeDtypeStruct((BX, S, S, OWN), F32),
        scratch_shapes=[pltpu.VMEM((4 * BX, 256, T), F32), pltpu.SemaphoreType.DMA((BX,))],
        compiler_params=pltpu.CompilerParams(vmem_limit_bytes=40 * 2**20),
        name="turn",
    )(info, inv)


def all_planes(cb, width_in, width_out, near, v, u0, u12, src, own_inv, halo_inv, store):
    u0[0, :, :width_in] = jnp.zeros((S, width_in), F32) if near is None else mm(cb, near[:, :width_in])[:S]
    for d in range(BX):
        u = mm(cb, v[d, :, :width_in])
        u0[d + 1, :, :width_in] = u[:S]
        u12[d, :, :width_in] = u[S:]
    masks = z_masks(width_in)
    slots = slot_iota(S)
    for d in range(BX):
        c = yz_terms(u12[d, :S, :width_in], u12[d, S:, :width_in], masks) + u0[d, :, :width_in]
        if d + 1 < BX:
            c = c + u0[d + 2, :, :width_in]
        pieces = [(lambda s, d=d: own_inv[d, s], c[:, :OWN] + src[d, :, :OWN])]
        if width_out > OWN:
            ch = c[:, OWN : OWN + T]
            if width_in == OWN + 2 * T:
                ch = low_high(slots, ch, c[:, OWN + T :])
            pieces.append((lambda s, d=d: halo_inv[d, s], ch + src[d, :, OWN:]))
        for at, x in zip((0, OWN), apply_inverse(pieces)):
            store(d, at, x)


def crit_step(cb, planes, v, near_u0, src, own_inv, crit_inv, halo_inv):
    masks = z_masks(OWN + 2 * T)
    u = {d: mm(cb, x) for d, x in v.items()}
    out = {}
    for d in planes:
        parts = []
        if d in u:
            parts.append(yz_terms(u[d][S : 2 * S], u[d][2 * S :], masks))
        if d == 0:
            if near_u0 is not None:
                parts.append(near_u0)
        elif d - 1 in u:
            parts.append(u[d - 1][:S])
        if d + 1 in u:
            parts.append(u[d + 1][:S])
        if src is not None:
            parts.append(src(d))
        c = functools.reduce(lambda a, b: a + b, parts)

        def tile(side, d=d):
            return (lambda s: crit_inv[d, side, s]) if d < 2 else (lambda s: halo_inv[d, s])

        pieces = [(lambda s, d=d: own_inv[d, s], c[:, :OWN]), (tile(0), c[:, OWN : OWN + T]), (tile(1), c[:, OWN + T :])]
        out[d] = jnp.concatenate(apply_inverse(pieces), axis=1)
    return out


def sides(info, a, b):
    odd, first, last = info[1], info[2], info[3]
    right = jnp.where(odd == 1, b, a)
    left = jnp.where(odd == 1, a, b)
    return jnp.where(last == 1, 0.0, right), jnp.where(first == 1, 0.0, left)


def put_edges(info, plane_value, pa, pb, d):
    odd = info[1]
    low, high = plane_value[:, :T], plane_value[:, OWN - T : OWN]
    pa[d] = jnp.where(odd == 1, low, high)
    pb[d] = jnp.where(odd == 1, high, low)


def first_kernel(
    info, coup, state, src_in, own_inv, pa1, pb1, g, ga, gb,
    v2, ea, eb, g4, g4a, g4b, halo_inv, crit_inv, src,
    v, vc, sc, u0, u12,
):
    flow, odd, first, last = info[0], info[1], info[2], info[3]
    cb = split_couplings(coup[...])
    slots = slot_iota(S)

    for s in range(S):
        for d in range(2):
            r, l = sides(info, pa1[pl.ds(d * 256 + s, S, stride=S), :], pb1[pl.ds(d * 256 + s, S, stride=S), :])
            crit_inv[d, 0, s] = r
            crit_inv[d, 1, s] = l
            halo_inv[d, s] = low_high(slots, r, l)
    for grp in range(3):
        for s in range(S):
            at = (2 + grp) * 256 + s
            r, l = sides(info, pa1[pl.ds(at, S, stride=S), :], pb1[pl.ds(at, S, stride=S), :])
            for q in range(4):
                x = jnp.where(slots == q, r, jnp.where(slots == (q + 3) % 4, l, 0.0))
                halo_inv[2 + 4 * grp + q, s] = pltpu.roll(x, T - CZ * q, 1) if q else x
    for s in range(S):
        at = 5 * 256 + s
        r, l = sides(info, pa1[pl.ds(at, S, stride=S), :], pb1[pl.ds(at, S, stride=S), :])
        halo_inv[14, s] = low_high(slots, r, l)
        halo_inv[15, s] = pltpu.roll(low_high(slots, l, r), 64, 1)

    for d in range(BX):
        p = plane_of(flow, d)
        v[d, :, :OWN] = state[p]
        src[d, :, :OWN] = src_in[p]
        if d < 2:
            at = SV0 + 2 * S * d
            r, l = sides(info, pa1[at : at + S], pb1[at : at + S])
            vc[d, :, :T] = r
            vc[d, :, T:] = l
            v[d, :, OWN:] = low_high(slots, r, l)
            r, l = sides(info, pa1[at + S : at + 2 * S], pb1[at + S : at + 2 * S])
            sc[d, :, :T] = r
            sc[d, :, T:] = l
            src[d, :, OWN:] = low_high(slots, r, l)
        else:
            at = SV0 + 2 * S + S * d
            r, l = sides(info, pa1[at : at + S], pb1[at : at + S])
            v[d, :, OWN:] = low_high(slots, r, l)
            src[d, :, OWN:] = pltpu.roll(low_high(slots, l, r), 64, 1)

    g_right, g_left = sides(info, ga[...], gb[...])
    use = flow == 0

    @pl.when(use)
    def _():
        def wide(own, combined, tiles, d):
            if d < 2:
                return jnp.concatenate([own, tiles[d]], axis=1)
            return jnp.concatenate([own, combined, combined], axis=1)

        vals = {d: wide(v[d, :, :OWN], v[d, :, OWN:], vc, d) for d in range(5)}
        near = mm(cb, jnp.concatenate([g[...], g_right, g_left], axis=1))[:S]
        for k in range(1, 5):
            vals = crit_step(
                cb, range(5 - k), vals, near,
                lambda d: wide(src[d, :, :OWN], src[d, :, OWN:], sc, d),
                own_inv, crit_inv, halo_inv,
            )
        top = vals[0]
        g4[...] = top[:, :OWN]
        g4a[...] = jnp.where(odd == 1, top[:, :T], top[:, OWN - T : OWN])
        g4b[...] = jnp.where(odd == 1, top[:, OWN - T : OWN], top[:, :T])

    @pl.when(jnp.logical_not(use))
    def _():
        g4[...] = jnp.zeros((S, OWN), F32)
        g4a[...] = jnp.zeros((S, T), F32)
        g4b[...] = jnp.zeros((S, T), F32)

    near = jnp.concatenate([g[...], low_high(slots, g_right, g_left)], axis=1)
    near = jnp.where(use, near, 0.0)

    def keep(d, at, x):
        v[d, :, at : at + x.shape[1]] = x

    def final(d, at, x):
        v2[d] = x
        put_edges(info, x, ea, eb, d)

    all_planes(cb, 640, 640, near, v, u0, u12, src, own_inv, halo_inv, keep)
    all_planes(cb, 640, 512, near, v, u0, u12, src, own_inv, halo_inv, final)


def later_kernel(second, *refs):
    if second:
        (info, coup, v_in, ea_in, eb_in, own_inv, halo_inv, crit_inv, src, g, ga, gb, h, ha, hb, pa2, pb2,
         v_out, ea, eb, halo_out, v, u0, u12) = refs
    else:
        (info, coup, v_in, ea_in, eb_in, own_inv, halo_out, src, h, ha, hb,
         v_out, g8, g8a, g8b, v, u0, u12) = refs
    flow, odd = info[0], info[1]
    cb = split_couplings(coup[...])
    slots = slot_iota(S)
    for d in range(BX):
        v[d, :, :OWN] = v_in[d]
        r, l = sides(info, ea_in[d], eb_in[d])
        v[d, :, OWN : OWN + T] = r
        v[d, :, OWN + T :] = l

    if second:
        for d in (0, 1, 14, 15):
            halo_out[d] = halo_inv[d]
        for grp in range(3):
            for s in range(S):
                at = grp * 256 + s
                r, l = sides(info, pa2[pl.ds(at, S, stride=S), :], pb2[pl.ds(at, S, stride=S), :])
                for q in range(4):
                    d = 2 + 4 * grp + q
                    x = jnp.where(slots == (q + 1) % 4, r, jnp.where(slots == (q + 2) % 4, l, 0.0))
                    halo_out[d, s] = halo_inv[d, s] + (pltpu.roll(x, T - CZ * q, 1) if q else x)

    h_right, h_left = sides(info, ha[...], hb[...])
    h_wide = jnp.concatenate([h[...], h_right, h_left], axis=1)

    if second:
        @pl.when(flow == 1)
        def _():
            near = mm(cb, h_wide)[:S]
            d1 = crit_step(cb, range(1), {}, near, None, own_inv, crit_inv, halo_inv)
            d2 = crit_step(cb, range(2), d1, near, None, own_inv, crit_inv, halo_inv)
            for d in range(2):
                v[d] = v[d] + d2[d]

    h_wide = jnp.where(flow == 1, h_wide, 0.0)
    near = h_wide
    if second:
        g_right, g_left = sides(info, ga[...], gb[...])
        near = jnp.where(flow == 1, h_wide, jnp.concatenate([g[...], g_right, g_left], axis=1))

    def narrow(x):
        return jnp.concatenate([x[:, :OWN], low_high(slots, x[:, OWN : OWN + T], x[:, OWN + T :])], axis=1)

    def keep(d, at, x):
        v[d, :, at : at + x.shape[1]] = x

    def final(d, at, x):
        v_out[d] = x
        if second:
            put_edges(info, x, ea, eb, d)
        elif d == 0:
            g8[...] = x
            low, high = x[:, :T], x[:, OWN - T :]
            g8a[...] = jnp.where(odd == 1, low, high)
            g8b[...] = jnp.where(odd == 1, high, low)

    all_planes(cb, 768, 640, near, v, u0, u12, src, own_inv, halo_out, keep)
    all_planes(cb, 640, 640, narrow(near), v, u0, u12, src, own_inv, halo_out, keep)
    all_planes(cb, 640, 512, narrow(h_wide), v, u0, u12, src, own_inv, halo_out, final)


def last_kernel(info, coup, v8, own_inv, halo_inv, crit_inv, g8, g8a, g8b, out):
    flow = info[0]
    for d in range(BX):
        out[plane_of(flow, d)] = v8[d]

    @pl.when(flow == 0)
    def _():
        cb = split_couplings(coup[...])
        r, l = sides(info, g8a[...], g8b[...])
        near = mm(cb, jnp.concatenate([g8[...], r, l], axis=1))[:S]
        vals = {}
        for j in range(1, 5):
            vals = crit_step(cb, range(j), vals, near, None, own_inv, crit_inv, halo_inv)
        for d in range(4):
            p = BX - 1 - d
            out[p] = v8[d] + vals[d][:, :OWN]


def call(kernel, name, ins, outs, scratch, limit=48):
    f = jax.ShapeDtypeStruct
    vm = pl.BlockSpec(memory_space=pltpu.VMEM)
    return pl.pallas_call(
        kernel,
        in_specs=[pl.BlockSpec(memory_space=pltpu.SMEM)] + [vm] * (len(ins) - 1),
        out_specs=[vm] * len(outs),
        out_shape=[f(s, F32) for s in outs],
        scratch_shapes=[pltpu.VMEM(s, F32) for s in scratch],
        compiler_params=pltpu.CompilerParams(vmem_limit_bytes=limit * 2**20),
        name=name,
    )(*ins)


def shards(state, src_in, inverse, couplings):
    count = lax.axis_size("gy")
    flow = lax.axis_index("flow")
    at = lax.axis_index("gy")
    info = jnp.stack([flow, at % 2, at == 0, at == count - 1]).astype(jnp.int32)
    coup = couplings.reshape(3 * S, S)
    inv = inverse.reshape(BX, S * S, OWN)

    mate = [i ^ 1 for i in range(count)]
    other = [(i + 1) % count if i % 2 else (i - 1) % count for i in range(count)]

    def swap_a(x):
        return lax.ppermute(x, "gy", list(enumerate(mate)))

    def swap_b(x):
        return lax.ppermute(x, "gy", list(enumerate(other)))

    def cross(x, to):
        pairs = [(f * count + i, (1 - f) * count + to[i]) for f in (0, 1) for i in range(count)]
        return lax.ppermute(x, ("flow", "gy"), pairs)

    def swap_f(x):
        return lax.ppermute(x, "flow", [(0, 1), (1, 0)])

    def hop(x, xa, xb):
        return swap_f(x), cross(xa, mate), cross(xb, other)

    pa1, pb1, pa2, pb2, g, ga, gb = pack(info, state, src_in, inv)
    pb1, pa1 = swap_b(pb1), swap_a(pa1)
    g, ga, gb = hop(g, ga, gb)
    pb2, pa2 = swap_b(pb2), swap_a(pa2)
    own_inv = turn(info, inv)

    plane, tile, tiles = (S, OWN), (S, T), (BX, S, T)
    field = (BX, S, OWN)
    v2, ea, eb, h, ha, hb, halo, crit, src = call(
        first_kernel, "first",
        [info, coup, state, src_in, own_inv, pa1, pb1, g, ga, gb],
        [field, tiles, tiles, plane, tile, tile, (BX, S, S, T), (2, 2, S, S, T), (BX, S, 640)],
        [(BX, S, 640), (2, S, 2 * T), (2, S, 2 * T), (BX + 2, S, 640), (BX, 2 * S, 640)],
    )
    h, ha, hb = hop(h, ha, hb)
    eb, ea = swap_b(eb), swap_a(ea)
    wide = [(BX, S, 768), (BX + 2, S, 768), (BX, 2 * S, 768)]
    v5, ea, eb, halo = call(
        functools.partial(later_kernel, True), "second",
        [info, coup, v2, ea, eb, own_inv, halo, crit, src, g, ga, gb, h, ha, hb, pa2, pb2],
        [field, tiles, tiles, (BX, S, S, T)], wide,
    )
    eb, ea = swap_b(eb), swap_a(ea)
    v8, g8, g8a, g8b = call(
        functools.partial(later_kernel, False), "third",
        [info, coup, v5, ea, eb, own_inv, halo, src, h, ha, hb],
        [field, plane, tile, tile], wide,
    )
    g8, g8a, g8b = hop(g8, g8a, g8b)
    (out,) = call(
        last_kernel, "last", [info, coup, v8, own_inv, halo, crit, g8, g8a, g8b], [field], [],
    )
    return out


def solution(mesh):
    return jax.shard_map(
        shards,
        mesh=mesh,
        in_specs=(P("flow", None, "gy"), P("flow", None, "gy"), P("flow", None, None, "gy"), P()),
        out_specs=P("flow", None, "gy"),
        check_vma=False,
    )
```

time: 403 us -> 112 us (0.28)
  the two profiles are of different devices: /device:TPU:29 before, /device:TPU:0 now
where the time goes in v1:
time: 112 us
  Pallas kernels  39.2 us (35%)
  waiting for transfers between devices  32.6 us (29%)
  starting transfers between devices  30.9 us (28%)
  local copies, waits for them, and re-layouts  8.74 us (8%)
    pallas_call x4, Pallas kernels, call(): pl.pallas_call(kernel, in_specs=[pl.BlockSpec(memory_space=pltpu.SMEM)] +...  31.4 us
    ppermute x6, waiting for transfers between devices, cross(): return lax.ppermute(x, ('flow', 'gy'), pairs)  28.2 us
    ppermute x4, starting transfers between devices, swap_b(): return lax.ppermute(x, 'gy', list(enumerate(other)))  17 us
    ppermute x6, starting transfers between devices, cross(): return lax.ppermute(x, ('flow', 'gy'), pairs)  12.6 us
    unnamed x14, local copies, waits for them, and re-layouts  8.74 us
    pallas_call x1, Pallas kernels, turn(): pl.pallas_call(turn_kernel, in_specs=[pl.BlockSpec(memory_space=pltpu.SME...  4.43 us
    ppermute x4, waiting for transfers between devices, swap_b(): return lax.ppermute(x, 'gy', list(enumerate(other)))  4.4 us
    pallas_call x1, Pallas kernels, pack(): pl.pallas_call(pack_kernel, in_specs=[pl.BlockSpec(memory_space=pltpu.SME...  3.42 us
  transfers between devices with their start and end apart: 17, of which 5 were waited for; matrix products, arithmetic and copies ran while one was open for 0% of the time, Pallas kernels for 12%

profile of v1, /device:TPU:0, one launch (start us, length us, event | category | flops | bytes accessed | tf_op | source)
XLA Modules:
  0.0 111.7 jit_solution(15032366396838588155)
XLA Ops:
  0.1 3.4 %copy-done.1 = f32[16,16,16,512]{3,2,1,0:T(8,128)S(1)} copy-done((f32[16,16,16,512]{3,2,1,0:T(8,128)S(1)}, f32[16,16,16,512]{3,2,1,0:T(8,128)}, u32[]{:S(2)}) %copy-start.1) | copy-done | bytes 8388632
  3.5 1.0 copy-done.2
  4.5 1.0 copy-done.4
  5.5 3.4 %pack.1 = (f32[1824,128]{1,0:T(8,128)S(1)}, f32[1824,128]{1,0:T(8,128)S(1)}, f32[768,128]{1,0:T(8,128)S(1)}, f32[768,128]{1,0:T(8,128)S(1)}, f32[16,512]{1,0:T(8...) custom-call(s32[4]{0:T(128)S(1)} %pad_add_fusion.info.refs_0_, f32[16,16,512]{2,1,0:T(8,128)S(1)} %copy-done.2, ...), custom_call_target="tpu_custom_call" | custom-call | tf_op jit(solution)/shard_map/pack/pallas_call | solution.py:135
  9.0 0.1 collective-permute-start
  9.1 9.1 %collective-permute-start.1 = (f32[1824,128]{1,0:T(8,128)S(1)}, f32[1824,128]{1,0:T(8,128)S(1)}, u32[]{:S(2)}, u32[]{:S(2)}) collective-permute-start(f32[1824,128]{1,0:T(8,128)S(1)} %get-tuple-element.30), channel_id=1, source_target_pairs={{0,63},{1,2},{2,1},{3,4},{4,3},{5,6},{6,5},{7,8},{8,7},{9,10},{10,... | collective-permute-start | bytes 2801672 | tf_op jit(solution)/shard_map/ppermute | solution.py:445
  18.2 0.9 collective-permute-start.11
  19.1 14.6 %collective-permute-done.3.ga.refs_10_ = f32[16,128]{1,0:T(8,128)S(1)} collective-permute-done((f32[16,128]{1,0:T(8,128)S(1)}, f32[16,128]{1,0:T(8,128)S(1)}, u32[]{:S(2)}, u32[]{:S(2)}) %collective-permute-start.3) | collective-permute-done | bytes 8224 | tf_op jit(solution)/shard_map/ppermute | solution.py:449
  33.7 8.5 %collective-permute-done.4.gb.refs_11_ = f32[16,128]{1,0:T(8,128)S(1)} collective-permute-done((f32[16,128]{1,0:T(8,128)S(1)}, f32[16,128]{1,0:T(8,128)S(1)}, u32[]{:S(2)}, u32[]{:S(2)}) %collective-permute-start.4) | collective-permute-done | bytes 8224 | tf_op jit(solution)/shard_map/ppermute | solution.py:449
  42.2 4.4 %turn.1.own_inv.refs_5_ = f32[16,16,16,512]{3,2,1,0:T(8,128)S(1)} custom-call(s32[4]{0:T(128)S(1)} %pad_add_fusion.info.refs_0_, f32[16,256,512]{2,1,0:T(8,128)} %bitcast.6), custom_call_target="tpu_custom_call" | custom-call | tf_op jit(solution)/shard_map/turn/pallas_call | solution.py:166
  46.6 3.3 %copy-done = f32[16,16,16,512]{3,2,1,0:T(8,128)} copy-done((f32[16,16,16,512]{3,2,1,0:T(8,128)}, f32[16,16,16,512]{3,2,1,0:T(8,128)S(1)}, u32[]{:S(2)}) %copy-start) | copy-done | bytes 8388632
  49.9 9.3 %first.1 = (f32[16,16,512]{2,1,0:T(8,128)S(1)}, f32[16,16,128]{2,1,0:T(8,128)S(1)}, f32[16,16,128]{2,1,0:T(8,128)S(1)}, f32[16,512]{1,0:T(8,128)S(1)}, f32[16,12...) custom-call(s32[4]{0:T(128)S(1)} %pad_add_fusion.info.refs_0_, ...), custom_call_target="tpu_custom_call" | custom-call | tf_op jit(solution)/shard_map/first/pallas_call | solution.py:419
  59.3 1.2 %collective-permute-start.6 = (f32[16,16,128]{2,1,0:T(8,128)S(1)}, f32[16,16,128]{2,1,0:T(8,128)S(1)}, u32[]{:S(2)}, u32[]{:S(2)}) collective-permute-start(f32[16,16,128]{2,1,0:T(8,128)S(1)} %get-tuple-element.36), channel_id=1, source_target_pairs={{0,63},{1,2},{2,1},{3,4},{4,3},{5,6},{6,5},{7,8},{8,7},{9,10},{10,... | collective-permute-start | bytes 393224 | tf_op jit(solution)/shard_map/ppermute | solution.py:445
  60.4 0.7 collective-permute-start.8
  61.1 6.2 %collective-permute-start.9 = (f32[16,128]{1,0:T(8,128)S(1)}, f32[16,128]{1,0:T(8,128)S(1)}, u32[]{:S(2)}, u32[]{:S(2)}) collective-permute-start(f32[16,128]{1,0:T(8,128)S(1)} %get-tuple-element.42), channel_id=1, source_target_pairs={{0,127},{1,66},{2,65},{3,68},{4,67},{5,70},{6,69},{7,72},{8,71},{9... | collective-permute-start | bytes 24584 | tf_op jit(solution)/shard_map/ppermute | solution.py:449
  67.3 2.3 %collective-permute-done.9.refs_14_.refs_10_ = f32[16,128]{1,0:T(8,128)S(1)} collective-permute-done((f32[16,128]{1,0:T(8,128)S(1)}, f32[16,128]{1,0:T(8,128)S(1)}, u32[]{:S(2)}, u32[]{:S(2)}) %collective-permute-start.9) | collective-permute-done | bytes 8224 | tf_op jit(solution)/shard_map/ppermute | solution.py:449
  69.7 8.9 %second.1 = (f32[16,16,512]{2,1,0:T(8,128)S(1)}, f32[16,16,128]{2,1,0:T(8,128)S(1)}, f32[16,16,128]{2,1,0:T(8,128)S(1)}, f32[16,16,16,128]{3,2,1,0:T(8,128)S(1)}) custom-call(s32[4]{0:T(128)S(1)} %pad_add_fusion.info.refs_0_, f32[48,16]{1,0:T(8,128)S(1)} %bitcast.9, f32[16,16,512]{2,1,0:T(8,128)S(1)} %get-tuple-element.34.refs_2_, ...), custom_call_target="tpu_custom_call" | custom-call | tf_op jit(solution)/shard_map/second/pallas_call | solution.py:419
  78.7 5.8 %collective-permute-start.13 = (f32[16,16,128]{2,1,0:T(8,128)S(1)}, f32[16,16,128]{2,1,0:T(8,128)S(1)}, u32[]{:S(2)}, u32[]{:S(2)}) collective-permute-start(f32[16,16,128]{2,1,0:T(8,128)S(1)} %get-tuple-element.47), channel_id=1, source_target_pairs={{0,63},{1,2},{2,1},{3,4},{4,3},{5,6},{6,5},{7,8},{8,7},{9,10},{10,... | collective-permute-start | bytes 393224 | tf_op jit(solution)/shard_map/ppermute | solution.py:445
  84.5 4.4 %collective-permute-done.13.refs_4_ = f32[16,16,128]{2,1,0:T(8,128)S(1)} collective-permute-done((f32[16,16,128]{2,1,0:T(8,128)S(1)}, f32[16,16,128]{2,1,0:T(8,128)S(1)}, u32[]{:S(2)}, u32[]{:S(2)}) %collective-permute-start.13) | collective-permute-done | bytes 131104 | tf_op jit(solution)/shard_map/ppermute | solution.py:445
  88.9 7.6 %third.1 = (f32[16,16,512]{2,1,0:T(8,128)S(1)}, f32[16,512]{1,0:T(8,128)S(1)}, f32[16,128]{1,0:T(8,128)S(1)}, f32[16,128]{1,0:T(8,128)S(1)}) custom-call(s32[4]{0:T(128)S(1)} %pad_add_fusion.info.refs_0_, f32[48,16]{1,0:T(8,128)S(1)} %bitcast.10, f32[16,16,512]{2,1,0:T(8,128)S(1)} %get-tuple-element.45.refs_2_, ...), custom_call_target="tpu_custom_call" | custom-call | tf_op jit(solution)/shard_map/third/pallas_call | solution.py:419
  96.5 1.1 %collective-permute-start.14 = (f32[16,512]{1,0:T(8,128)S(1)}, f32[16,512]{1,0:T(8,128)S(1)}, u32[]{:S(2)}, u32[]{:S(2)}) collective-permute-start(f32[16,512]{1,0:T(8,128)S(1)} %get-tuple-element.50), channel_id=1, source_target_pairs={{0,64},{64,0},{1,65},{65,1},{2,66},{66,2},{3,67},{67,3},{4,68},{68... | collective-permute-start | bytes 98312 | tf_op jit(solution)/shard_map/ppermute | solution.py:452
  97.6 5.8 %collective-permute-start.16 = (f32[16,128]{1,0:T(8,128)S(1)}, f32[16,128]{1,0:T(8,128)S(1)}, u32[]{:S(2)}, u32[]{:S(2)}) collective-permute-start(f32[16,128]{1,0:T(8,128)S(1)} %get-tuple-element.52), channel_id=1, source_target_pairs={{0,127},{1,66},{2,65},{3,68},{4,67},{5,70},{6,69},{7,72},{8,71},{9... | collective-permute-start | bytes 24584 | tf_op jit(solution)/shard_map/ppermute | solution.py:449
  103.4 2.7 %collective-permute-done.16.g8b = f32[16,128]{1,0:T(8,128)S(1)} collective-permute-done((f32[16,128]{1,0:T(8,128)S(1)}, f32[16,128]{1,0:T(8,128)S(1)}, u32[]{:S(2)}, u32[]{:S(2)}) %collective-permute-start.16) | collective-permute-done | bytes 8224 | tf_op jit(solution)/shard_map/ppermute | solution.py:449
  106.1 5.5 %last.1 = f32[16,16,512]{2,1,0:T(8,128)} custom-call(s32[4]{0:T(128)S(1)} %pad_add_fusion.info.refs_0_, f32[48,16]{1,0:T(8,128)S(1)} %bitcast.11, f32[16,16,512]{2,1,0:T(8,128)S(1)} %get-tuple-element.49.v8, f32[16,16,16,512]{3,2,1,0:T(8,128)} %copy-done, f32[16,16,16,128]{3,2,1,0:T(8,128)S(1)} %get-tuple-element.48.refs_6_.halo_inv, ...), custom_call_target="tpu_custom_call" | custom-call | tf_op jit(solution)/shard_map/last/pallas_call | solution.py:419
  (31 shorter events, 0.2 us)
Async XLA Ops:
  0.1 3.4 %copy-start.1 = (f32[16,16,16,512]{3,2,1,0:T(8,128)S(1)}, f32[16,16,16,512]{3,2,1,0:T(8,128)}, u32[]{:S(2)}) copy-start(f32[16,16,16,512]{3,2,1,0:T(8,128)} %param.6) | copy-start | bytes 25165828
  3.5 1.0 copy-start.2
  4.5 1.0 copy-start.4
  9.0 40.9 %collective-permute-start = (f32[1824,128]{1,0:T(8,128)S(1)}, f32[1824,128]{1,0:T(8,128)S(1)}, u32[]{:S(2)}, u32[]{:S(2)}) collective-permute-start(f32[1824,128]{1,0:T(8,128)S(1)} %get-tuple-element.29), channel_id=1, source_target_pairs={{0,1},{1,0},{2,3},{3,2},{4,5},{5,4},{6,7},{7,6},{8,9},{9,8},{10,11... | collective-permute-start | bytes 2801672 | tf_op jit(solution)/shard_map/ppermute | solution.py:442
  9.1 40.9 %collective-permute-start.1 = (f32[1824,128]{1,0:T(8,128)S(1)}, f32[1824,128]{1,0:T(8,128)S(1)}, u32[]{:S(2)}, u32[]{:S(2)}) collective-permute-start(f32[1824,128]{1,0:T(8,128)S(1)} %get-tuple-element.30), channel_id=1, source_target_pairs={{0,63},{1,2},{2,1},{3,4},{4,3},{5,6},{6,5},{7,8},{8,7},{9,10},{10,... | collective-permute-start | bytes 2801672 | tf_op jit(solution)/shard_map/ppermute | solution.py:445
  18.2 42.2 %collective-permute-start.10 = (f32[768,128]{1,0:T(8,128)S(1)}, f32[768,128]{1,0:T(8,128)S(1)}, u32[]{:S(2)}, u32[]{:S(2)}) collective-permute-start(f32[768,128]{1,0:T(8,128)S(1)} %get-tuple-element.43), channel_id=1, source_target_pairs={{0,1},{1,0},{2,3},{3,2},{4,5},{5,4},{6,7},{7,6},{8,9},{9,8},{10,11... | collective-permute-start | bytes 1179656 | tf_op jit(solution)/shard_map/ppermute | solution.py:442
  18.2 42.9 %collective-permute-start.11 = (f32[768,128]{1,0:T(8,128)S(1)}, f32[768,128]{1,0:T(8,128)S(1)}, u32[]{:S(2)}, u32[]{:S(2)}) collective-permute-start(f32[768,128]{1,0:T(8,128)S(1)} %get-tuple-element.44), channel_id=1, source_target_pairs={{0,63},{1,2},{2,1},{3,4},{4,3},{5,6},{6,5},{7,8},{8,7},{9,10},{10,... | collective-permute-start | bytes 1179656 | tf_op jit(solution)/shard_map/ppermute | solution.py:445
  19.1 14.6 %collective-permute-start.3 = (f32[16,128]{1,0:T(8,128)S(1)}, f32[16,128]{1,0:T(8,128)S(1)}, u32[]{:S(2)}, u32[]{:S(2)}) collective-permute-start(f32[16,128]{1,0:T(8,128)S(1)} %get-tuple-element.32), channel_id=1, source_target_pairs={{0,65},{1,64},{2,67},{3,66},{4,69},{5,68},{6,71},{7,70},{8,73},{9,... | collective-permute-start | bytes 24584 | tf_op jit(solution)/shard_map/ppermute | solution.py:449
  33.7 8.5 %collective-permute-start.4 = (f32[16,128]{1,0:T(8,128)S(1)}, f32[16,128]{1,0:T(8,128)S(1)}, u32[]{:S(2)}, u32[]{:S(2)}) collective-permute-start(f32[16,128]{1,0:T(8,128)S(1)} %get-tuple-element.33), channel_id=1, source_target_pairs={{0,127},{1,66},{2,65},{3,68},{4,67},{5,70},{6,69},{7,72},{8,71},{9... | collective-permute-start | bytes 24584 | tf_op jit(solution)/shard_map/ppermute | solution.py:449
  42.2 7.7 %copy-start.3 = (f32[16,16,512]{2,1,0:T(8,128)S(1)}, f32[16,16,512]{2,1,0:T(8,128)}, u32[]{:S(2)}) copy-start(f32[16,16,512]{2,1,0:T(8,128)} %state.3) | copy-start | bytes 1572868
  42.2 7.7 %copy-start.5 = (f32[16,16,512]{2,1,0:T(8,128)S(1)}, f32[16,16,512]{2,1,0:T(8,128)}, u32[]{:S(2)}) copy-start(f32[16,16,512]{2,1,0:T(8,128)} %src_in.1) | copy-start | bytes 1572868
  42.2 7.8 %copy-start.6 = (f32[3,16,16]{2,1,0:T(8,128)S(1)}, f32[3,16,16]{2,1,0:T(8,128)}, u32[]{:S(2)}) copy-start(f32[3,16,16]{2,1,0:T(8,128)} %param.7) | copy-start | bytes 9220
  42.2 7.7 %collective-permute-start.2 = (f32[16,512]{1,0:T(8,128)S(1)}, f32[16,512]{1,0:T(8,128)S(1)}, u32[]{:S(2)}, u32[]{:S(2)}) collective-permute-start(f32[16,512]{1,0:T(8,128)S(1)} %get-tuple-element.31), channel_id=1, source_target_pairs={{0,64},{64,0},{1,65},{65,1},{2,66},{66,2},{3,67},{67,3},{4,68},{68... | collective-permute-start | bytes 98312 | tf_op jit(solution)/shard_map/ppermute | solution.py:452
  46.6 3.3 %copy-start = (f32[16,16,16,512]{3,2,1,0:T(8,128)}, f32[16,16,16,512]{3,2,1,0:T(8,128)S(1)}, u32[]{:S(2)}) copy-start(f32[16,16,16,512]{3,2,1,0:T(8,128)S(1)} %turn.1.own_inv.refs_5_) | copy-start | bytes 25165828
  59.3 10.4 %collective-permute-start.5 = (f32[16,16,128]{2,1,0:T(8,128)S(1)}, f32[16,16,128]{2,1,0:T(8,128)S(1)}, u32[]{:S(2)}, u32[]{:S(2)}) collective-permute-start(f32[16,16,128]{2,1,0:T(8,128)S(1)} %get-tuple-element.35), channel_id=1, source_target_pairs={{0,1},{1,0},{2,3},{3,2},{4,5},{5,4},{6,7},{7,6},{8,9},{9,8},{10,11... | collective-permute-start | bytes 393224 | tf_op jit(solution)/shard_map/ppermute | solution.py:442
  59.3 10.4 %collective-permute-start.6 = (f32[16,16,128]{2,1,0:T(8,128)S(1)}, f32[16,16,128]{2,1,0:T(8,128)S(1)}, u32[]{:S(2)}, u32[]{:S(2)}) collective-permute-start(f32[16,16,128]{2,1,0:T(8,128)S(1)} %get-tuple-element.36), channel_id=1, source_target_pairs={{0,63},{1,2},{2,1},{3,4},{4,3},{5,6},{6,5},{7,8},{8,7},{9,10},{10,... | collective-permute-start | bytes 393224 | tf_op jit(solution)/shard_map/ppermute | solution.py:445
  60.4 9.2 %collective-permute-start.7 = (f32[16,512]{1,0:T(8,128)S(1)}, f32[16,512]{1,0:T(8,128)S(1)}, u32[]{:S(2)}, u32[]{:S(2)}) collective-permute-start(f32[16,512]{1,0:T(8,128)S(1)} %get-tuple-element.40), channel_id=1, source_target_pairs={{0,64},{64,0},{1,65},{65,1},{2,66},{66,2},{3,67},{67,3},{4,68},{68... | collective-permute-start | bytes 98312 | tf_op jit(solution)/shard_map/ppermute | solution.py:452
  60.4 6.8 %collective-permute-start.8 = (f32[16,128]{1,0:T(8,128)S(1)}, f32[16,128]{1,0:T(8,128)S(1)}, u32[]{:S(2)}, u32[]{:S(2)}) collective-permute-start(f32[16,128]{1,0:T(8,128)S(1)} %get-tuple-element.41), channel_id=1, source_target_pairs={{0,65},{1,64},{2,67},{3,66},{4,69},{5,68},{6,71},{7,70},{8,73},{9,... | collective-permute-start | bytes 24584 | tf_op jit(solution)/shard_map/ppermute | solution.py:449
  61.1 8.5 %collective-permute-start.9 = (f32[16,128]{1,0:T(8,128)S(1)}, f32[16,128]{1,0:T(8,128)S(1)}, u32[]{:S(2)}, u32[]{:S(2)}) collective-permute-start(f32[16,128]{1,0:T(8,128)S(1)} %get-tuple-element.42), channel_id=1, source_target_pairs={{0,127},{1,66},{2,65},{3,68},{4,67},{5,70},{6,69},{7,72},{8,71},{9... | collective-permute-start | bytes 24584 | tf_op jit(solution)/shard_map/ppermute | solution.py:449
  78.6 5.9 %collective-permute-start.12 = (f32[16,16,128]{2,1,0:T(8,128)S(1)}, f32[16,16,128]{2,1,0:T(8,128)S(1)}, u32[]{:S(2)}, u32[]{:S(2)}) collective-permute-start(f32[16,16,128]{2,1,0:T(8,128)S(1)} %get-tuple-element.46), channel_id=1, source_target_pairs={{0,1},{1,0},{2,3},{3,2},{4,5},{5,4},{6,7},{7,6},{8,9},{9,8},{10,11... | collective-permute-start | bytes 393224 | tf_op jit(solution)/shard_map/ppermute | solution.py:442
  78.7 10.2 %collective-permute-start.13 = (f32[16,16,128]{2,1,0:T(8,128)S(1)}, f32[16,16,128]{2,1,0:T(8,128)S(1)}, u32[]{:S(2)}, u32[]{:S(2)}) collective-permute-start(f32[16,16,128]{2,1,0:T(8,128)S(1)} %get-tuple-element.47), channel_id=1, source_target_pairs={{0,63},{1,2},{2,1},{3,4},{4,3},{5,6},{6,5},{7,8},{8,7},{9,10},{10,... | collective-permute-start | bytes 393224 | tf_op jit(solution)/shard_map/ppermute | solution.py:445
  96.5 9.6 %collective-permute-start.14 = (f32[16,512]{1,0:T(8,128)S(1)}, f32[16,512]{1,0:T(8,128)S(1)}, u32[]{:S(2)}, u32[]{:S(2)}) collective-permute-start(f32[16,512]{1,0:T(8,128)S(1)} %get-tuple-element.50), channel_id=1, source_target_pairs={{0,64},{64,0},{1,65},{65,1},{2,66},{66,2},{3,67},{67,3},{4,68},{68... | collective-permute-start | bytes 98312 | tf_op jit(solution)/shard_map/ppermute | solution.py:452
  97.6 5.8 %collective-permute-start.15 = (f32[16,128]{1,0:T(8,128)S(1)}, f32[16,128]{1,0:T(8,128)S(1)}, u32[]{:S(2)}, u32[]{:S(2)}) collective-permute-start(f32[16,128]{1,0:T(8,128)S(1)} %get-tuple-element.51), channel_id=1, source_target_pairs={{0,65},{1,64},{2,67},{3,66},{4,69},{5,68},{6,71},{7,70},{8,73},{9,... | collective-permute-start | bytes 24584 | tf_op jit(solution)/shard_map/ppermute | solution.py:449
  97.6 8.5 %collective-permute-start.16 = (f32[16,128]{1,0:T(8,128)S(1)}, f32[16,128]{1,0:T(8,128)S(1)}, u32[]{:S(2)}, u32[]{:S(2)}) collective-permute-start(f32[16,128]{1,0:T(8,128)S(1)} %get-tuple-element.52), channel_id=1, source_target_pairs={{0,127},{1,66},{2,65},{3,68},{4,67},{5,70},{6,69},{7,72},{8,71},{9... | collective-permute-start | bytes 24584 | tf_op jit(solution)/shard_map/ppermute | solution.py:449

commit v2 on v1

v2 whole, which is shorter than its diff:
```python
import functools

import jax
import jax.numpy as jnp
from jax import lax
from jax.experimental import pallas as pl
from jax.experimental.pallas import tpu as pltpu
from jax.sharding import PartitionSpec as P

S = 16
BX = 16
CZ = 32
OWN = 512
T = 128
F32 = jnp.float32
BF16 = jnp.bfloat16

SV0 = 6 * 256
PAY1 = SV0 + 18 * S
SV1 = 5 * 256
PAY2 = SV1 + 2 * S
PACK_LIMIT = 58
TURN_LIMIT = 40


def position():
    at = lax.axis_index("gy")
    return lax.axis_index("flow"), at % 2, at == 0, at == lax.axis_size("gy") - 1


def slot_iota(rows):
    return lax.broadcasted_iota(jnp.int32, (rows, T), 1) // CZ


def plane_of(flow, d):
    return jnp.where(flow == 1, d, BX - 1 - d)


def split_couplings(c):
    hi = c.astype(BF16)
    lo = (c - hi.astype(F32)).astype(BF16)
    return jnp.concatenate([hi, hi, lo], axis=1)


def mm(cb, v):
    hi = v.astype(BF16)
    lo = (v - hi.astype(F32)).astype(BF16)
    return jnp.dot(cb, jnp.concatenate([hi, lo, hi], axis=0), preferred_element_type=F32)


def z_masks(width):
    z = lax.broadcasted_iota(jnp.int32, (S, width), 1) % CZ
    return z != 0, z != CZ - 1


def yz_terms(u1, u2, masks):
    width = u1.shape[1]
    below, above = masks
    y = pltpu.roll(u1, CZ, 1) + pltpu.roll(u1, width - CZ, 1)
    z = jnp.where(below, pltpu.roll(u2, 1, 1), 0.0) + jnp.where(above, pltpu.roll(u2, width - 1, 1), 0.0)
    return y + z


def apply_inverse(pieces):
    out = []
    for get, c in pieces:
        acc = get(0) * c[0:1, :]
        for s in range(1, S):
            acc = acc + get(s) * c[s : s + 1, :]
        out.append(acc)
    return out


def low_high(slots, right, left):
    return jnp.where(slots < 2, right, left)


def pack_kernel(state, src, inv, pa1, pb1, pa2, pb2, edge, next1, se, re, s1, s2, sem, osem):
    flow, odd, _, _ = position()
    place = (1 - odd, odd)
    started = []

    def fetch(source, target):
        c = pltpu.make_async_copy(source, target, sem.at[len(started)])
        c.start()
        started.append(c)
        return c

    field = [fetch(x.at[:, :, pl.ds(384 * side, T)], y.at[side]) for x, y in ((state, se), (src, re)) for side in (0, 1)]
    planes = {}
    for d in range(2, BX):
        for side in (0, 1):
            planes[d, side] = fetch(inv.at[plane_of(flow, d), :, pl.ds(384 * side, T)], edge.at[2 * d - 4 + side])
    rest = []
    for side in (0, 1):
        at = pl.ds(384 * side, T)
        at2 = pl.ds(T + T * side, T)
        rest.append(fetch(inv.at[plane_of(flow, 1), :, at2], next1.at[side]))
        rest.append(fetch(inv.at[plane_of(flow, 0), :, at], s1.at[place[side], pl.ds(0, 256)]))
        rest.append(fetch(inv.at[plane_of(flow, 1), :, at], s1.at[place[side], pl.ds(256, 256)]))
        rest.append(fetch(inv.at[plane_of(flow, 0), :, at2], s2.at[place[side], pl.ds(0, 256)]))
        rest.append(fetch(src.at[plane_of(flow, 0), :, at2], s2.at[place[side], pl.ds(SV1, S)]))
    sent = []

    def send(scratch, outs, row, count):
        for j in range(2):
            c = pltpu.make_async_copy(
                scratch.at[j, pl.ds(row, count)], outs[j].at[pl.ds(row, count)], osem.at[len(sent)]
            )
            c.start()
            sent.append(c)

    for c in field:
        c.wait()
    slots = slot_iota(S)
    for side in (0, 1):
        j = place[side]
        row = SV0
        for d in range(BX):
            p = plane_of(flow, d)
            v, r = se[side, p], re[side, p]
            if d < 2:
                s1[j, row : row + S] = v
                s1[j, row + S : row + 2 * S] = r
                row += 2 * S
            else:
                s1[j, row : row + S] = jnp.where((slots >= 2) if side else (slots < 2), v, pltpu.roll(r, 64, 1))
                row += S
        s2[j, SV1 + S : SV1 + 2 * S] = re[side, plane_of(flow, 2)]
    send(s1, (pa1, pb1), SV0, 18 * S)

    slots8 = slot_iota(8)
    for grp in range(3):
        for q in range(4):
            for side in (0, 1):
                planes[2 + 4 * grp + q, side].wait()

        def rows(i, _, grp=grp):
            at = pl.multiple_of(i * 8, 8)
            for side in (0, 1):
                one = two = None
                for q in range(4):
                    x = edge[2 * (4 * grp + q) + side, pl.ds(at, 8), :]
                    x = pltpu.roll(x, CZ * q, 1) if q else x
                    one = x if one is None else jnp.where(slots8 == ((3 if side else 0) + q) % 4, x, one)
                    two = x if two is None else jnp.where(slots8 == ((2 if side else 1) + q) % 4, x, two)
                s1[place[side], pl.ds((2 + grp) * 256 + at, 8), :] = one
                s2[place[side], pl.ds((2 + grp) * 256 + at, 8), :] = two
            return 0

        lax.fori_loop(0, 32, rows, 0, unroll=8)
        send(s1, (pa1, pb1), (2 + grp) * 256, 256)
        send(s2, (pa2, pb2), (2 + grp) * 256, 256)
    for d in (14, 15):
        for side in (0, 1):
            planes[d, side].wait()
    for c in rest:
        c.wait()
    send(s1, (pa1, pb1), 0, 512)
    send(s2, (pa2, pb2), 0, 256)

    def rows(i, _):
        at = pl.multiple_of(i * 8, 8)
        for side in (0, 1):
            j = place[side]
            a = edge[24 + side, pl.ds(at, 8), :]
            b = edge[26 + side, pl.ds(at, 8), :]
            s1[j, pl.ds(5 * 256 + at, 8), :] = jnp.where((slots8 >= 2) if side else (slots8 < 2), a, pltpu.roll(b, 64, 1))
            s2[j, pl.ds(256 + at, 8), :] = jnp.where(
                slots8 == (3 if side else 0), next1[side, pl.ds(at, 8), :], edge[side, pl.ds(at, 8), :]
            )
        return 0

    lax.fori_loop(0, 32, rows, 0, unroll=8)
    send(s1, (pa1, pb1), 5 * 256, 256)
    send(s2, (pa2, pb2), 256, 256)
    send(s2, (pa2, pb2), SV1, 2 * S)
    for c in sent:
        c.wait()


def pack(state, src, inv):
    f = jax.ShapeDtypeStruct
    hbm = pl.BlockSpec(memory_space=pltpu.HBM)
    return pl.pallas_call(
        pack_kernel,
        in_specs=[hbm] * 3,
        out_specs=[hbm] * 4,
        out_shape=[f((PAY1, T), F32)] * 2 + [f((PAY2, T), F32)] * 2,
        scratch_shapes=[
            pltpu.VMEM((2 * BX - 4, 256, T), F32),
            pltpu.VMEM((2, 256, T), F32),
            pltpu.VMEM((2, BX, S, T), F32),
            pltpu.VMEM((2, BX, S, T), F32),
            pltpu.VMEM((2, PAY1, T), F32),
            pltpu.VMEM((2, PAY2, T), F32),
            pltpu.SemaphoreType.DMA((42,)),
            pltpu.SemaphoreType.DMA((24,)),
        ],
        compiler_params=pltpu.CompilerParams(vmem_limit_bytes=PACK_LIMIT * 2**20),
        name="pack",
    )(state, src, inv)


def turn_kernel(inv, out, buf, sem):
    flow = position()[0]

    def copy(i):
        d, tile = i // 4, i % 4
        return pltpu.make_async_copy(
            inv.at[plane_of(flow, d), :, pl.ds(tile * T, T)], buf.at[i], sem.at[d]
        )

    for i in range(4 * BX):
        copy(i).start()
    for d in range(BX):
        for tile in range(4):
            copy(4 * d + tile).wait()
        for tile in range(4):
            for s in range(S):
                out[d, s, :, tile * T : (tile + 1) * T] = buf[4 * d + tile, pl.ds(s, S, stride=S), :]


def turn(inv):
    return pl.pallas_call(
        turn_kernel,
        in_specs=[pl.BlockSpec(memory_space=pltpu.HBM)],
        out_specs=pl.BlockSpec(memory_space=pltpu.VMEM),
        out_shape=jax.ShapeDtypeStruct((BX, S, S, OWN), F32),
        scratch_shapes=[pltpu.VMEM((4 * BX, 256, T), F32), pltpu.SemaphoreType.DMA((BX,))],
        compiler_params=pltpu.CompilerParams(vmem_limit_bytes=TURN_LIMIT * 2**20),
        name="turn",
    )(inv)


def all_planes(cb, width_in, width_out, near, v, u0, u12, src, own_inv, halo_inv, store):
    u0[0, :, :width_in] = jnp.zeros((S, width_in), F32) if near is None else mm(cb, near[:, :width_in])[:S]
    for d in range(BX):
        u = mm(cb, v[d, :, :width_in])
        u0[d + 1, :, :width_in] = u[:S]
        u12[d, :, :width_in] = u[S:]
    masks = z_masks(width_in)
    slots = slot_iota(S)
    for d in range(BX):
        c = yz_terms(u12[d, :S, :width_in], u12[d, S:, :width_in], masks) + u0[d, :, :width_in]
        if d + 1 < BX:
            c = c + u0[d + 2, :, :width_in]
        pieces = [(lambda s, d=d: own_inv[d, s], c[:, :OWN] + src[d, :, :OWN])]
        if width_out > OWN:
            ch = c[:, OWN : OWN + T]
            if width_in == OWN + 2 * T:
                ch = low_high(slots, ch, c[:, OWN + T :])
            pieces.append((lambda s, d=d: halo_inv[d, s], ch + src[d, :, OWN:]))
        for at, x in zip((0, OWN), apply_inverse(pieces)):
            store(d, at, x)


def fit(x, width):
    have = x.shape[1]
    if have == width:
        return x
    side = (width - OWN) // 2
    return jnp.concatenate([x[:, : OWN + side], x[:, have - side :]], axis=1)


def crit_step(cb, planes, v, near_u0, src, inv, wide=()):
    u = {d: mm(cb, x) for d, x in v.items()}
    out = {}
    for d in planes:
        width = OWN + (4 if d in wide else 2) * T
        parts = []
        if d in u:
            masks = z_masks(u[d].shape[1])
            parts.append(yz_terms(u[d][S : 2 * S], u[d][2 * S :], masks))
        if d == 0:
            parts.append(near_u0)
        elif d - 1 in u:
            parts.append(u[d - 1][:S])
        if d + 1 in u:
            parts.append(u[d + 1][:S])
        if src is not None:
            parts.append(src(d))
        c = functools.reduce(lambda a, b: a + b, [fit(x, width) for x in parts])
        order = (0, 1, 2, -2, -1) if d in wide else (0, 1, -1)
        pieces = []
        at = 0
        for i in order:
            n = T if i else OWN
            pieces.append((inv(d, i), c[:, at : at + n]))
            at += n
        out[d] = jnp.concatenate(apply_inverse(pieces), axis=1)
    return out


def sides(a, b):
    _, odd, first, last = position()
    right = jnp.where(odd == 1, b, a)
    left = jnp.where(odd == 1, a, b)
    return jnp.where(last, 0.0, right), jnp.where(first, 0.0, left)


def put_edges(x, pa, pb, at, first=0, count=1):
    odd = position()[1]
    low = x[:, first * T : (first + count) * T]
    high = x[:, OWN - (first + count) * T : OWN - first * T]
    pa[at] = jnp.where(odd == 1, low, high)
    pb[at] = jnp.where(odd == 1, high, low)


def first_kernel(
    coup, state, src_in, own_inv, pa1, pb1, g, ga, gb,
    v2, ea, eb, h, ha, hb, halo_inv, crit_inv, src, sc,
    v, vc, u0, u12,
):
    flow = position()[0]
    cb = split_couplings(coup[...])
    slots = slot_iota(S)

    for s in range(S):
        for d in range(2):
            r, l = sides(pa1[pl.ds(d * 256 + s, S, stride=S), :], pb1[pl.ds(d * 256 + s, S, stride=S), :])
            crit_inv[d, 0, s] = r
            crit_inv[d, 1, s] = l
            halo_inv[d, s] = low_high(slots, r, l)
    for grp in range(3):
        for s in range(S):
            at = (2 + grp) * 256 + s
            r, l = sides(pa1[pl.ds(at, S, stride=S), :], pb1[pl.ds(at, S, stride=S), :])
            for q in range(4):
                x = jnp.where(slots == q, r, jnp.where(slots == (q + 3) % 4, l, 0.0))
                halo_inv[2 + 4 * grp + q, s] = pltpu.roll(x, T - CZ * q, 1) if q else x
    for s in range(S):
        at = 5 * 256 + s
        r, l = sides(pa1[pl.ds(at, S, stride=S), :], pb1[pl.ds(at, S, stride=S), :])
        halo_inv[14, s] = low_high(slots, r, l)
        halo_inv[15, s] = pltpu.roll(low_high(slots, l, r), 64, 1)

    for d in range(BX):
        p = plane_of(flow, d)
        v[d, :, :OWN] = state[p]
        src[d, :, :OWN] = src_in[p]
        if d < 2:
            at = SV0 + 2 * S * d
            r, l = sides(pa1[at : at + S], pb1[at : at + S])
            vc[d, :, :T] = r
            vc[d, :, T:] = l
            v[d, :, OWN:] = low_high(slots, r, l)
            r, l = sides(pa1[at + S : at + 2 * S], pb1[at + S : at + 2 * S])
            sc[d, :, :T] = r
            sc[d, :, T:] = l
            src[d, :, OWN:] = low_high(slots, r, l)
        else:
            at = SV0 + 2 * S + S * d
            r, l = sides(pa1[at : at + S], pb1[at : at + S])
            v[d, :, OWN:] = low_high(slots, r, l)
            src[d, :, OWN:] = pltpu.roll(low_high(slots, l, r), 64, 1)

    g_right, g_left = sides(ga[...], gb[...])
    use = flow == 0

    @pl.when(use)
    def _():
        def wide(own, combined, tiles, d):
            if d < 2:
                return jnp.concatenate([own, tiles[d]], axis=1)
            return jnp.concatenate([own, combined, combined], axis=1)

        def inv(d, i):
            if i == 0:
                return lambda s: own_inv[d, s]
            return (lambda s: crit_inv[d, int(i < 0), s]) if d < 2 else (lambda s: halo_inv[d, s])

        vals = {d: wide(v[d, :, :OWN], v[d, :, OWN:], vc, d) for d in range(5)}
        near = mm(cb, jnp.concatenate([g[...], g_right, g_left], axis=1))[:S]
        for k in range(1, 5):
            vals = crit_step(
                cb, range(5 - k), vals, near, lambda d: wide(src[d, :, :OWN], src[d, :, OWN:], sc, d), inv
            )
        top = vals[0][:, :OWN]
        h[...] = top
        put_edges(top, ha, hb, slice(None), 0, 2)

    @pl.when(jnp.logical_not(use))
    def _():
        h[...] = jnp.zeros((S, OWN), F32)
        ha[...] = jnp.zeros((S, 2 * T), F32)
        hb[...] = jnp.zeros((S, 2 * T), F32)

    near = jnp.concatenate([g[...], low_high(slots, g_right, g_left)], axis=1)
    near = jnp.where(use, near, 0.0)

    def keep(d, at, x):
        v[d, :, at : at + x.shape[1]] = x

    def final(d, at, x):
        v2[d] = x
        put_edges(x, ea, eb, d)
        if d < 2:
            put_edges(x, ea, eb, BX + d, 1)

    all_planes(cb, 640, 640, near, v, u0, u12, src, own_inv, halo_inv, keep)
    all_planes(cb, 640, 512, near, v, u0, u12, src, own_inv, halo_inv, final)


def load_field(v, v_in, ea_in, eb_in):
    for d in range(BX):
        v[d, :, :OWN] = v_in[d]
        r, l = sides(ea_in[d], eb_in[d])
        v[d, :, OWN : OWN + T] = r
        v[d, :, OWN + T :] = l


def narrow(x, slots):
    x = fit(x, OWN + 2 * T)
    return jnp.concatenate([x[:, :OWN], low_high(slots, x[:, OWN : OWN + T], x[:, OWN + T :])], axis=1)


def second_kernel(
    coup, v_in, ea_in, eb_in, own_inv, halo_in, crit_inv, src, g, ga, gb, h, ha, hb, pa2, pb2,
    v_out, ea, eb, halo_inv,
    v, u0, u12,
):
    flow = position()[0]
    cb = split_couplings(coup[...])
    slots = slot_iota(S)
    load_field(v, v_in, ea_in, eb_in)

    def taken(at):
        return sides(pa2[pl.ds(at, S, stride=S), :], pb2[pl.ds(at, S, stride=S), :])

    for d in (0, 1, 14, 15):
        halo_inv[d] = halo_in[d]
    for grp in range(3):
        for s in range(S):
            r, l = taken((2 + grp) * 256 + s)
            for q in range(4):
                d = 2 + 4 * grp + q
                x = jnp.where(slots == (q + 1) % 4, r, jnp.where(slots == (q + 2) % 4, l, 0.0))
                halo_inv[d, s] = halo_in[d, s] + (pltpu.roll(x, T - CZ * q, 1) if q else x)

    h_wide = jnp.concatenate([h[...], *sides(ha[...], hb[...])], axis=1)

    @pl.when(flow == 1)
    def _():
        def inv(d, i):
            return (lambda s: crit_inv[d, int(i < 0), s]) if i else (lambda s: own_inv[d, s])

        near = mm(cb, fit(h_wide, OWN + 2 * T))[:S]
        d1 = crit_step(cb, range(1), {}, near, None, inv)
        d2 = crit_step(cb, range(2), d1, near, None, inv)
        for d in range(2):
            v[d] = v[d] + d2[d]

    h_near = jnp.where(flow == 1, fit(h_wide, OWN + 2 * T), 0.0)
    g_wide = jnp.concatenate([g[...], *sides(ga[...], gb[...])], axis=1)
    near = jnp.where(flow == 1, h_near, g_wide)

    def keep(d, at, x):
        v[d, :, at : at + x.shape[1]] = x

    def final(d, at, x):
        v_out[d] = x
        put_edges(x, ea, eb, d)

    all_planes(cb, 768, 640, near, v, u0, u12, src, own_inv, halo_inv, keep)
    all_planes(cb, 640, 640, narrow(near, slots), v, u0, u12, src, own_inv, halo_inv, keep)
    all_planes(cb, 640, 512, narrow(h_near, slots), v, u0, u12, src, own_inv, halo_inv, final)


def cone_kernel(
    coup, v_in, ea_in, eb_in, own_inv, halo_inv, crit_inv, src, sc, h, ha, hb, pa2, pb2,
    g8, g8a, g8b,
    far, third,
):
    flow = position()[0]
    cb = split_couplings(coup[...])
    slots = slot_iota(S)

    def taken(at):
        return sides(pa2[pl.ds(at, S, stride=S), :], pb2[pl.ds(at, S, stride=S), :])

    h_wide = jnp.concatenate([h[...], *sides(ha[...], hb[...])], axis=1)

    @pl.when(flow == 1)
    def _():
        for s in range(S):
            far[0, 0, s], far[0, 1, s] = taken(s)
            r, l = taken(256 + s)
            far[1, 0, s] = jnp.where(slots == 0, r, 0.0)
            far[1, 1, s] = jnp.where(slots == 3, l, 0.0)
            third[0, s] = jnp.where(slots < 2, halo_inv[2, s], jnp.where(slots == 2, r, 0.0))
            third[1, s] = jnp.where(slots >= 2, halo_inv[2, s], jnp.where(slots == 1, l, 0.0))

        def inv(d, i):
            if i == 0:
                return lambda s: own_inv[d, s]
            if abs(i) == 2:
                return lambda s: far[d, int(i < 0), s]
            if d < 2:
                return lambda s: crit_inv[d, int(i < 0), s]
            return (lambda s: third[int(i < 0), s]) if d == 2 else (lambda s: halo_inv[d, s])

        near = mm(cb, h_wide)[:S]
        d1 = crit_step(cb, range(1), {}, near, None, inv, (0,))
        d2 = crit_step(cb, range(2), d1, near, None, inv, (0, 1))
        vals = {}
        for d in range(7):
            r, l = sides(ea_in[d], eb_in[d])
            if d < 2:
                r2, l2 = sides(ea_in[BX + d], eb_in[BX + d])
                vals[d] = jnp.concatenate([v_in[d], r, r2, l2, l], axis=1) + d2[d]
            else:
                vals[d] = jnp.concatenate([v_in[d], r, l], axis=1)

        def source(d):
            own = src[d, :, :OWN]
            if d > 2:
                return jnp.concatenate([own, src[d, :, OWN:], src[d, :, OWN:]], axis=1)
            if d == 2:
                return jnp.concatenate([own, *sides(pa2[SV1 + S : SV1 + 2 * S], pb2[SV1 + S : SV1 + 2 * S])], axis=1)
            if d == 1:
                return jnp.concatenate([own, sc[1]], axis=1)
            r, l = sides(pa2[SV1 : SV1 + S], pb2[SV1 : SV1 + S])
            return jnp.concatenate([own, sc[0, :, :T], r, l, sc[0, :, T:]], axis=1)

        for k in range(3, 9):
            vals = crit_step(cb, range(9 - k), vals, near, source, inv, (0,) if k == 3 else ())
        top = vals[0][:, :OWN]
        g8[...] = top
        put_edges(top, g8a, g8b, slice(None))

    @pl.when(flow == 0)
    def _():
        g8[...] = jnp.zeros((S, OWN), F32)
        g8a[...] = jnp.zeros((S, T), F32)
        g8b[...] = jnp.zeros((S, T), F32)


def third_kernel(
    coup, v_in, ea_in, eb_in, own_inv, halo_inv, crit_inv, src, h, ha, hb, g8, g8a, g8b,
    out,
    v, u0, u12, done, sem,
):
    flow = position()[0]
    cb = split_couplings(coup[...])
    slots = slot_iota(S)
    load_field(v, v_in, ea_in, eb_in)
    g_wide = jnp.concatenate([g8[...], *sides(g8a[...], g8b[...])], axis=1)

    @pl.when(flow == 0)
    def _():
        def inv(d, i):
            return (lambda s: crit_inv[d, int(i < 0), s]) if i else (lambda s: own_inv[d, s])

        v[0] = v[0] + crit_step(cb, range(1), {}, mm(cb, g_wide)[:S], None, inv)[0]

    h_wide = fit(jnp.concatenate([h[...], *sides(ha[...], hb[...])], axis=1), OWN + 2 * T)
    near = jnp.where(flow == 1, h_wide, g_wide)

    def keep(d, at, x):
        v[d, :, at : at + x.shape[1]] = x

    sent = []

    def final(d, at, x):
        done[d] = x
        c = pltpu.make_async_copy(done.at[d], out.at[plane_of(flow, d)], sem.at[d])
        c.start()
        sent.append(c)

    all_planes(cb, 768, 640, near, v, u0, u12, src, own_inv, halo_inv, keep)
    all_planes(cb, 640, 640, narrow(near, slots), v, u0, u12, src, own_inv, halo_inv, keep)
    all_planes(cb, 640, 512, narrow(near, slots), v, u0, u12, src, own_inv, halo_inv, final)
    for c in sent:
        c.wait()


def call(kernel, name, ins, outs, scratch, out_space=pltpu.VMEM, limit=16):
    f = jax.ShapeDtypeStruct
    vm = pl.BlockSpec(memory_space=pltpu.VMEM)
    return pl.pallas_call(
        kernel,
        in_specs=[vm] * len(ins),
        out_specs=[pl.BlockSpec(memory_space=out_space)] * len(outs),
        out_shape=[f(s, F32) for s in outs],
        scratch_shapes=[pltpu.VMEM(s, F32) if isinstance(s, tuple) else s for s in scratch],
        compiler_params=pltpu.CompilerParams(vmem_limit_bytes=limit * 2**20),
        name=name,
    )(*ins)


def shards(state, src_in, inverse, couplings):
    count = lax.axis_size("gy")
    flow = lax.axis_index("flow")
    at = lax.axis_index("gy")
    coup = couplings.reshape(3 * S, S)
    inv = inverse.reshape(BX, S * S, OWN)

    mate = [i ^ 1 for i in range(count)]
    other = [(i + 1) % count if i % 2 else (i - 1) % count for i in range(count)]

    def swap_a(x):
        return lax.ppermute(x, "gy", list(enumerate(mate)))

    def swap_b(x):
        return lax.ppermute(x, "gy", list(enumerate(other)))

    def cross(x, to):
        pairs = [(f * count + i, (1 - f) * count + to[i]) for f in (0, 1) for i in range(count)]
        return lax.ppermute(x, ("flow", "gy"), pairs)

    def swap_f(x):
        return lax.ppermute(x, "flow", [(0, 1), (1, 0)])

    def hop(x, xa, xb):
        return swap_f(x), cross(xa, mate), cross(xb, other)

    g = jnp.where(flow == 1, state[0], state[BX - 1])
    low, high = g[:, :T], g[:, OWN - T :]
    ga, gb = jnp.where(at % 2 == 1, low, high), jnp.where(at % 2 == 1, high, low)
    g, ga, gb = hop(g, ga, gb)
    pa1, pb1, pa2, pb2 = pack(state, src_in, inv)
    pb1, pa1 = swap_b(pb1), swap_a(pa1)
    own_inv = turn(inv)
    pa1, g, ga, gb, own_inv, pa2, pb2 = lax.optimization_barrier((pa1, g, ga, gb, own_inv, pa2, pb2))
    pb2, pa2 = swap_b(pb2), swap_a(pa2)

    plane, tile, tiles = (S, OWN), (S, T), (BX, S, T)
    field = (BX, S, OWN)
    v2, ea, eb, h, ha, hb, halo, crit, src, sc = call(
        first_kernel, "first",
        [coup, state, src_in, own_inv, pa1, pb1, g, ga, gb],
        [field, (BX + 2, S, T), (BX + 2, S, T), plane, (S, 2 * T), (S, 2 * T), (BX, S, S, T), (2, 2, S, S, T),
         (BX, S, 640), (2, S, 2 * T)],
        [(BX, S, 640), (2, S, 2 * T), (BX + 2, S, 640), (BX, 2 * S, 640)],
    )
    h, ha, hb, ea, eb, pa2 = lax.optimization_barrier((h, ha, hb, ea, eb, pa2))
    eb, ea = swap_b(eb), swap_a(ea)
    h, ha = swap_f(h), cross(ha, mate)
    ea, hb = lax.optimization_barrier((ea, hb))
    hb = cross(hb, other)
    wide = [(BX, S, 768), (BX + 2, S, 768), (BX, 2 * S, 768)]
    v5, ea5, eb5, halo = call(
        second_kernel, "second",
        [coup, v2, ea, eb, own_inv, halo, crit, src, g, ga, gb, h, ha, hb, pa2, pb2],
        [field, tiles, tiles, (BX, S, S, T)], wide,
    )
    g8, g8a, g8b = call(
        cone_kernel, "cone",
        [coup, v2, ea, eb, own_inv, halo, crit, src, sc, h, ha, hb, pa2, pb2],
        [plane, tile, tile], [(2, 2, S, S, T), (2, S, S, T)],
    )
    eb5, ea5 = swap_b(eb5), swap_a(ea5)
    g8, g8a, g8b = hop(g8, g8a, g8b)
    (out,) = call(
        third_kernel, "third",
        [coup, v5, ea5, eb5, own_inv, halo, crit, src, h, ha, hb, g8, g8a, g8b],
        [field], wide + [(BX, S, OWN), pltpu.SemaphoreType.DMA((BX,))], pltpu.HBM,
    )
    return out


def solution(mesh):
    return jax.shard_map(
        shards,
        mesh=mesh,
        in_specs=(P("flow", None, "gy"), P("flow", None, "gy"), P("flow", None, None, "gy"), P()),
        out_specs=P("flow", None, "gy"),
        check_vma=False,
    )
```

time: 112 us -> 73.6 us (0.66)
  Pallas kernels: 39.2 us -> 24.2 us
  waiting for transfers between devices: 32.6 us -> 18.6 us
  local copies, waits for them, and re-layouts: 8.74 us -> 0.02 us
    pallas_call x6, Pallas kernels: 39.2 us -> 24.2 us  [the longest x4 15.4 us: call(): pl.pallas_call(kernel, in_specs=[vm] * len(ins), out_specs=[pl.BlockSpec(...]
    ppermute x6, waiting for transfers between devices: 28.2 us -> 13.2 us  [cross(): return lax.ppermute(x, ('flow', 'gy'), pairs)]
    unnamed x14 -> x10, local copies, waits for them, and re-layouts: 8.74 us -> 0.02 us
    ppermute x6, starting transfers between devices: 12.6 us -> 6.71 us  [cross(): return lax.ppermute(x, ('flow', 'gy'), pairs)]
    ppermute x3, starting transfers between devices: 1.14 us -> 4.83 us  [swap_f(): return lax.ppermute(x, 'flow', [(0, 1), (1, 0)])]
    ppermute x4, starting transfers between devices: 17 us -> 18.3 us  [swap_b(): return lax.ppermute(x, 'gy', list(enumerate(other)))]
  transfers between devices with their start and end apart: 17 -> 17, of which waited for: 5 -> 8; matrix products, arithmetic and copies ran while one was open for 0% -> 0% of each run, Pallas kernels for 12% -> 12%
where the time goes in v2:
time: 73.6 us; the launch traced here: 73.5 us
  starting transfers between devices  30.3 us (41%)
  Pallas kernels  24.2 us (33%)
  waiting for transfers between devices  18.6 us (25%)
    ppermute x4, starting transfers between devices, swap_b(): return lax.ppermute(x, 'gy', list(enumerate(other)))  18.3 us
    pallas_call x4, Pallas kernels, call(): pl.pallas_call(kernel, in_specs=[vm] * len(ins), out_specs=[pl.BlockSpec(...  15.4 us
    ppermute x6, waiting for transfers between devices, cross(): return lax.ppermute(x, ('flow', 'gy'), pairs)  13.2 us
    ppermute x6, starting transfers between devices, cross(): return lax.ppermute(x, ('flow', 'gy'), pairs)  6.71 us
    pallas_call x1, Pallas kernels, pack(): pl.pallas_call(pack_kernel, in_specs=[hbm] * 3, out_specs=[hbm] * 4, out_...  4.84 us
    ppermute x3, starting transfers between devices, swap_f(): return lax.ppermute(x, 'flow', [(0, 1), (1, 0)])  4.83 us
    ppermute x4, waiting for transfers between devices, swap_b(): return lax.ppermute(x, 'gy', list(enumerate(other)))  4.27 us
    pallas_call x1, Pallas kernels, turn(): pl.pallas_call(turn_kernel, in_specs=[pl.BlockSpec(memory_space=pltpu.HBM...  3.99 us
  transfers between devices with their start and end apart: 17, of which 8 were waited for; matrix products, arithmetic and copies ran while one was open for 0% of the time, Pallas kernels for 12%

profile of v2, /device:TPU:0, one launch (start us, length us, event | category | flops | bytes accessed | tf_op | source)
XLA Modules:
  0.0 73.5 jit_solution(15951948164849745366)
XLA Ops:
  0.0 4.8 %pack.1 = (f32[1824,128]{1,0:T(8,128)}, f32[1824,128]{1,0:T(8,128)}, f32[1312,128]{1,0:T(8,128)}, f32[1312,128]{1,0:T(8,128)}) custom-call(f32[16,16,512]{2,1,0:T(8,128)} %state.3, f32[16,16,512]{2,1,0:T(8,128)} %src_in.1, f32[16,256,512]{2,1,0:T(8,128)} %bitcast.8), custom_call_target="tpu_custom_call" | custom-call | tf_op jit(solution)/shard_map/pack/pallas_call | solution.py:185
  4.9 9.1 %collective-permute-start.4 = (f32[1824,128]{1,0:T(8,128)}, f32[1824,128]{1,0:T(8,128)S(1)}, u32[]{:S(2)}, u32[]{:S(2)}) collective-permute-start(f32[1824,128]{1,0:T(8,128)} %get-tuple-element.46), channel_id=1, source_target_pairs={{0,63},{1,2},{2,1},{3,4},{4,3},{5,6},{6,5},{7,8},{8,7},{9,10},{10,... | collective-permute-start | bytes 2801672 | tf_op jit(solution)/shard_map/ppermute | solution.py:606
  14.1 0.7 collective-permute-start.1
  14.8 0.1 collective-permute-start.2
  14.9 4.0 %turn.1.own_inv = f32[16,16,16,512]{3,2,1,0:T(8,128)S(1)} custom-call(f32[16,256,512]{2,1,0:T(8,128)} %bitcast.9), custom_call_target="tpu_custom_call" | custom-call | tf_op jit(solution)/shard_map/turn/pallas_call | solution.py:225
  18.9 5.2 %collective-permute-done.3.gb = f32[16,128]{1,0:T(8,128)S(1)} collective-permute-done((f32[16,128]{1,0:T(8,128)S(1)}, f32[16,128]{1,0:T(8,128)S(1)}, u32[]{:S(2)}, u32[]{:S(2)}) %collective-permute-start.3) | collective-permute-done | bytes 8224 | tf_op jit(solution)/shard_map/ppermute | solution.py:610
  24.1 1.8 %collective-permute-done.2.ga = f32[16,128]{1,0:T(8,128)S(1)} collective-permute-done((f32[16,128]{1,0:T(8,128)S(1)}, f32[16,128]{1,0:T(8,128)S(1)}, u32[]{:S(2)}, u32[]{:S(2)}) %collective-permute-start.2) | collective-permute-done | bytes 8224 | tf_op jit(solution)/shard_map/ppermute | solution.py:610
  25.9 1.0 %collective-permute-done.1.g = f32[16,512]{1,0:T(8,128)S(1)} collective-permute-done((f32[16,512]{1,0:T(8,128)S(1)}, f32[16,512]{1,0:T(8,128)S(1)}, u32[]{:S(2)}, u32[]{:S(2)}) %collective-permute-start.1) | collective-permute-done | bytes 32800 | tf_op jit(solution)/shard_map/ppermute | solution.py:613
  26.9 0.2 collective-permute-start.5
  27.1 0.9 %collective-permute-start.11 = (f32[1312,128]{1,0:T(8,128)S(1)}, f32[1312,128]{1,0:T(8,128)S(1)}, u32[]{:S(2)}, u32[]{:S(2)}) collective-permute-start(f32[1312,128]{1,0:T(8,128)S(1)} %copy-done.3), channel_id=1, source_target_pairs={{0,63},{1,2},{2,1},{3,4},{4,3},{5,6},{6,5},{7,8},{8,7},{9,10},{10,... | collective-permute-start | bytes 2015240 | tf_op jit(solution)/shard_map/ppermute | solution.py:606
  28.0 4.8 %first.1 = (f32[16,16,512]{2,1,0:T(8,128)S(1)}, f32[18,16,128]{2,1,0:T(8,128)S(1)}, f32[18,16,128]{2,1,0:T(8,128)S(1)}, f32[16,512]{1,0:T(8,128)S(1)}, f32[16,25...) custom-call(f32[48,16]{1,0:T(8,128)S(1)} %bitcast.4, ...), custom_call_target="tpu_custom_call" | custom-call | tf_op jit(solution)/shard_map/first/pallas_call | solution.py:581
  32.8 6.7 %collective-permute-start.7 = (f32[18,16,128]{2,1,0:T(8,128)S(1)}, f32[18,16,128]{2,1,0:T(8,128)S(1)}, u32[]{:S(2)}, u32[]{:S(2)}) collective-permute-start(f32[18,16,128]{2,1,0:T(8,128)S(1)} %get-tuple-element.60), channel_id=1, source_target_pairs={{0,63},{1,2},{2,1},{3,4},{4,3},{5,6},{6,5},{7,8},{8,7},{9,10},{10,... | collective-permute-start | bytes 442376 | tf_op jit(solution)/shard_map/ppermute | solution.py:606
  39.5 0.1 collective-permute-start.8
  39.7 1.2 %collective-permute-start.10 = (f32[16,256]{1,0:T(8,128)S(1)}, f32[16,256]{1,0:T(8,128)S(1)}, u32[]{:S(2)}, u32[]{:S(2)}) collective-permute-start(f32[16,256]{1,0:T(8,128)S(1)} %get-tuple-element.66), channel_id=1, source_target_pairs={{0,127},{1,66},{2,65},{3,68},{4,67},{5,70},{6,69},{7,72},{8,71},{9... | collective-permute-start | bytes 49160 | tf_op jit(solution)/shard_map/ppermute | solution.py:610
  40.9 2.5 %collective-permute-done.11.pb2 = f32[1312,128]{1,0:T(8,128)S(1)} collective-permute-done((f32[1312,128]{1,0:T(8,128)S(1)}, f32[1312,128]{1,0:T(8,128)S(1)}, u32[]{:S(2)}, u32[]{:S(2)}) %collective-permute-start.11) | collective-permute-done | bytes 671776 | tf_op jit(solution)/shard_map/ppermute | solution.py:606
  43.3 0.1 collective-permute-done.8.h
  43.5 1.8 %collective-permute-done.7.eb_in = f32[18,16,128]{2,1,0:T(8,128)S(1)} collective-permute-done((f32[18,16,128]{2,1,0:T(8,128)S(1)}, f32[18,16,128]{2,1,0:T(8,128)S(1)}, u32[]{:S(2)}, u32[]{:S(2)}) %collective-permute-start.7) | collective-permute-done | bytes 147488 | tf_op jit(solution)/shard_map/ppermute | solution.py:606
  45.3 3.1 %collective-permute-done.10.hb = f32[16,256]{1,0:T(8,128)S(1)} collective-permute-done((f32[16,256]{1,0:T(8,128)S(1)}, f32[16,256]{1,0:T(8,128)S(1)}, u32[]{:S(2)}, u32[]{:S(2)}) %collective-permute-start.10) | collective-permute-done | bytes 16416 | tf_op jit(solution)/shard_map/ppermute | solution.py:610
  48.4 4.9 %second.1 = (f32[16,16,512]{2,1,0:T(8,128)S(1)}, f32[16,16,128]{2,1,0:T(8,128)S(1)}, f32[16,16,128]{2,1,0:T(8,128)S(1)}, f32[16,16,16,128]{3,2,1,0:T(8,128)S(1)}) custom-call(f32[48,16]{1,0:T(8,128)S(1)} %bitcast.5, f32[16,16,512]{2,1,0:T(8,128)S(1)} %get-tuple-element.50.v_in, f32[18,16,128]{2,1,0:T(8,128)S(1)} %collective-permute-done.6.ea_in, ...), custom_call_target="tpu_custom_call" | custom-call | tf_op jit(solution)/shard_map/second/pallas_call | solution.py:581
  53.4 1.7 %collective-permute-start.13 = (f32[16,16,128]{2,1,0:T(8,128)S(1)}, f32[16,16,128]{2,1,0:T(8,128)S(1)}, u32[]{:S(2)}, u32[]{:S(2)}) collective-permute-start(f32[16,16,128]{2,1,0:T(8,128)S(1)} %get-tuple-element.71), channel_id=1, source_target_pairs={{0,63},{1,2},{2,1},{3,4},{4,3},{5,6},{6,5},{7,8},{8,7},{9,10},{10,... | collective-permute-start | bytes 393224 | tf_op jit(solution)/shard_map/ppermute | solution.py:606
  55.2 4.0 %collective-permute-start.14 = (f32[16,512]{1,0:T(8,128)S(1)}, f32[16,512]{1,0:T(8,128)S(1)}, u32[]{:S(2)}, u32[]{:S(2)}) collective-permute-start(f32[16,512]{1,0:T(8,128)S(1)} %get-tuple-element.74), channel_id=1, source_target_pairs={{0,64},{64,0},{1,65},{65,1},{2,66},{66,2},{3,67},{67,3},{4,68},{68... | collective-permute-start | bytes 98312 | tf_op jit(solution)/shard_map/ppermute | solution.py:613
  59.2 5.4 %collective-permute-start.16 = (f32[16,128]{1,0:T(8,128)S(1)}, f32[16,128]{1,0:T(8,128)S(1)}, u32[]{:S(2)}, u32[]{:S(2)}) collective-permute-start(f32[16,128]{1,0:T(8,128)S(1)} %get-tuple-element.76), channel_id=1, source_target_pairs={{0,127},{1,66},{2,65},{3,68},{4,67},{5,70},{6,69},{7,72},{8,71},{9... | collective-permute-start | bytes 24584 | tf_op jit(solution)/shard_map/ppermute | solution.py:610
  64.6 3.1 %collective-permute-done.16.g8b = f32[16,128]{1,0:T(8,128)S(1)} collective-permute-done((f32[16,128]{1,0:T(8,128)S(1)}, f32[16,128]{1,0:T(8,128)S(1)}, u32[]{:S(2)}, u32[]{:S(2)}) %collective-permute-start.16) | collective-permute-done | bytes 8224 | tf_op jit(solution)/shard_map/ppermute | solution.py:610
  67.7 5.6 %third.1 = f32[16,16,512]{2,1,0:T(8,128)} custom-call(f32[48,16]{1,0:T(8,128)S(1)} %bitcast.7, f32[16,16,512]{2,1,0:T(8,128)S(1)} %get-tuple-element.69.v_in, f32[16,16,128]{2,1,0:T(8,128)S(1)} %collective-permute-done.12.ea_in, f32[16,16,128]{2,1,0:T(8,128)S(1)} %collective-permute-done.13.eb_in, f32[16,16,16,512]{3,2,1,0:T(8,128)S(1)} %turn.1.own_inv, ...), custom_call_target="tpu_custom_call" | custom-call | tf_op jit(solution)/shard_map/third/pallas_call | solution.py:581
  (28 shorter events, 0.4 us)
Async XLA Ops:
  0.0 14.1 %copy-start = (f32[16,16,512]{2,1,0:T(8,128)S(1)}, f32[16,16,512]{2,1,0:T(8,128)}, u32[]{:S(2)}) copy-start(f32[16,16,512]{2,1,0:T(8,128)} %state.3) | copy-start | bytes 1572868
  4.9 22.0 %collective-permute-start = (f32[1824,128]{1,0:T(8,128)}, f32[1824,128]{1,0:T(8,128)S(1)}, u32[]{:S(2)}, u32[]{:S(2)}) collective-permute-start(f32[1824,128]{1,0:T(8,128)} %get-tuple-element.41), channel_id=1, source_target_pairs={{0,1},{1,0},{2,3},{3,2},{4,5},{5,4},{6,7},{7,6},{8,9},{9,8},{10,11... | collective-permute-start | bytes 2801672 | tf_op jit(solution)/shard_map/ppermute | solution.py:603
  4.9 23.0 %collective-permute-start.4 = (f32[1824,128]{1,0:T(8,128)}, f32[1824,128]{1,0:T(8,128)S(1)}, u32[]{:S(2)}, u32[]{:S(2)}) collective-permute-start(f32[1824,128]{1,0:T(8,128)} %get-tuple-element.46), channel_id=1, source_target_pairs={{0,63},{1,2},{2,1},{3,4},{4,3},{5,6},{6,5},{7,8},{8,7},{9,10},{10,... | collective-permute-start | bytes 2801672 | tf_op jit(solution)/shard_map/ppermute | solution.py:606
  14.1 12.8 %collective-permute-start.1 = (f32[16,512]{1,0:T(8,128)S(1)}, f32[16,512]{1,0:T(8,128)S(1)}, u32[]{:S(2)}, u32[]{:S(2)}) collective-permute-start(f32[16,512]{1,0:T(8,128)S(1)} %select_bitcast_fusion), channel_id=1, source_target_pairs={{0,64},{64,0},{1,65},{65,1},{2,66},{66,2},{3,67},{67,3},{4,68},{68... | collective-permute-start | bytes 98312 | tf_op jit(solution)/shard_map/ppermute | solution.py:613
  14.8 9.3 %collective-permute-start.3 = (f32[16,128]{1,0:T(8,128)S(1)}, f32[16,128]{1,0:T(8,128)S(1)}, u32[]{:S(2)}, u32[]{:S(2)}) collective-permute-start(f32[16,128]{1,0:T(8,128)S(1)} %get-tuple-element.77), channel_id=1, source_target_pairs={{0,127},{1,66},{2,65},{3,68},{4,67},{5,70},{6,69},{7,72},{8,71},{9... | collective-permute-start | bytes 24584 | tf_op jit(solution)/shard_map/ppermute | solution.py:610
  14.8 12.1 %copy-start.4 = (f32[1312,128]{1,0:T(8,128)S(1)}, f32[1312,128]{1,0:T(8,128)}, u32[]{:S(2)}) copy-start(f32[1312,128]{1,0:T(8,128)} %get-tuple-element.56) | copy-start | bytes 2015236
  14.8 12.3 %copy-start.3 = (f32[1312,128]{1,0:T(8,128)S(1)}, f32[1312,128]{1,0:T(8,128)}, u32[]{:S(2)}) copy-start(f32[1312,128]{1,0:T(8,128)} %get-tuple-element.68) | copy-start | bytes 2015236
  14.8 13.2 %copy-start.1 = (f32[16,16,512]{2,1,0:T(8,128)S(1)}, f32[16,16,512]{2,1,0:T(8,128)}, u32[]{:S(2)}) copy-start(f32[16,16,512]{2,1,0:T(8,128)} %src_in.1) | copy-start | bytes 1572868
  14.8 13.2 %copy-start.2 = (f32[3,16,16]{2,1,0:T(8,128)S(1)}, f32[3,16,16]{2,1,0:T(8,128)}, u32[]{:S(2)}) copy-start(f32[3,16,16]{2,1,0:T(8,128)} %param.7) | copy-start | bytes 9220
  14.8 11.1 %collective-permute-start.2 = (f32[16,128]{1,0:T(8,128)S(1)}, f32[16,128]{1,0:T(8,128)S(1)}, u32[]{:S(2)}, u32[]{:S(2)}) collective-permute-start(f32[16,128]{1,0:T(8,128)S(1)} %get-tuple-element.78), channel_id=1, source_target_pairs={{0,65},{1,64},{2,67},{3,66},{4,69},{5,68},{6,71},{7,70},{8,73},{9,... | collective-permute-start | bytes 24584 | tf_op jit(solution)/shard_map/ppermute | solution.py:610
  26.9 5.9 %collective-permute-start.5 = (f32[1312,128]{1,0:T(8,128)S(1)}, f32[1312,128]{1,0:T(8,128)S(1)}, u32[]{:S(2)}, u32[]{:S(2)}) collective-permute-start(f32[1312,128]{1,0:T(8,128)S(1)} %copy-done.4), channel_id=1, source_target_pairs={{0,1},{1,0},{2,3},{3,2},{4,5},{5,4},{6,7},{7,6},{8,9},{9,8},{10,11... | collective-permute-start | bytes 2015240 | tf_op jit(solution)/shard_map/ppermute | solution.py:603
  27.1 16.3 %collective-permute-start.11 = (f32[1312,128]{1,0:T(8,128)S(1)}, f32[1312,128]{1,0:T(8,128)S(1)}, u32[]{:S(2)}, u32[]{:S(2)}) collective-permute-start(f32[1312,128]{1,0:T(8,128)S(1)} %copy-done.3), channel_id=1, source_target_pairs={{0,63},{1,2},{2,1},{3,4},{4,3},{5,6},{6,5},{7,8},{8,7},{9,10},{10,... | collective-permute-start | bytes 2015240 | tf_op jit(solution)/shard_map/ppermute | solution.py:606
  32.7 6.9 %collective-permute-start.6 = (f32[18,16,128]{2,1,0:T(8,128)S(1)}, f32[18,16,128]{2,1,0:T(8,128)S(1)}, u32[]{:S(2)}, u32[]{:S(2)}) collective-permute-start(f32[18,16,128]{2,1,0:T(8,128)S(1)} %get-tuple-element.57), channel_id=1, source_target_pairs={{0,1},{1,0},{2,3},{3,2},{4,5},{5,4},{6,7},{7,6},{8,9},{9,8},{10,11... | collective-permute-start | bytes 442376 | tf_op jit(solution)/shard_map/ppermute | solution.py:603
  32.8 12.4 %collective-permute-start.7 = (f32[18,16,128]{2,1,0:T(8,128)S(1)}, f32[18,16,128]{2,1,0:T(8,128)S(1)}, u32[]{:S(2)}, u32[]{:S(2)}) collective-permute-start(f32[18,16,128]{2,1,0:T(8,128)S(1)} %get-tuple-element.60), channel_id=1, source_target_pairs={{0,63},{1,2},{2,1},{3,4},{4,3},{5,6},{6,5},{7,8},{8,7},{9,10},{10,... | collective-permute-start | bytes 442376 | tf_op jit(solution)/shard_map/ppermute | solution.py:606
  39.5 4.0 %collective-permute-start.8 = (f32[16,512]{1,0:T(8,128)S(1)}, f32[16,512]{1,0:T(8,128)S(1)}, u32[]{:S(2)}, u32[]{:S(2)}) collective-permute-start(f32[16,512]{1,0:T(8,128)S(1)} %get-tuple-element.64), channel_id=1, source_target_pairs={{0,64},{64,0},{1,65},{65,1},{2,66},{66,2},{3,67},{67,3},{4,68},{68... | collective-permute-start | bytes 98312 | tf_op jit(solution)/shard_map/ppermute | solution.py:613
  39.7 3.7 %collective-permute-start.9 = (f32[16,256]{1,0:T(8,128)S(1)}, f32[16,256]{1,0:T(8,128)S(1)}, u32[]{:S(2)}, u32[]{:S(2)}) collective-permute-start(f32[16,256]{1,0:T(8,128)S(1)} %get-tuple-element.65), channel_id=1, source_target_pairs={{0,65},{1,64},{2,67},{3,66},{4,69},{5,68},{6,71},{7,70},{8,73},{9,... | collective-permute-start | bytes 49160 | tf_op jit(solution)/shard_map/ppermute | solution.py:610
  39.7 8.7 %collective-permute-start.10 = (f32[16,256]{1,0:T(8,128)S(1)}, f32[16,256]{1,0:T(8,128)S(1)}, u32[]{:S(2)}, u32[]{:S(2)}) collective-permute-start(f32[16,256]{1,0:T(8,128)S(1)} %get-tuple-element.66), channel_id=1, source_target_pairs={{0,127},{1,66},{2,65},{3,68},{4,67},{5,70},{6,69},{7,72},{8,71},{9... | collective-permute-start | bytes 49160 | tf_op jit(solution)/shard_map/ppermute | solution.py:610
  53.3 14.4 %collective-permute-start.12 = (f32[16,16,128]{2,1,0:T(8,128)S(1)}, f32[16,16,128]{2,1,0:T(8,128)S(1)}, u32[]{:S(2)}, u32[]{:S(2)}) collective-permute-start(f32[16,16,128]{2,1,0:T(8,128)S(1)} %get-tuple-element.70), channel_id=1, source_target_pairs={{0,1},{1,0},{2,3},{3,2},{4,5},{5,4},{6,7},{7,6},{8,9},{9,8},{10,11... | collective-permute-start | bytes 393224 | tf_op jit(solution)/shard_map/ppermute | solution.py:603
  53.4 14.3 %collective-permute-start.13 = (f32[16,16,128]{2,1,0:T(8,128)S(1)}, f32[16,16,128]{2,1,0:T(8,128)S(1)}, u32[]{:S(2)}, u32[]{:S(2)}) collective-permute-start(f32[16,16,128]{2,1,0:T(8,128)S(1)} %get-tuple-element.71), channel_id=1, source_target_pairs={{0,63},{1,2},{2,1},{3,4},{4,3},{5,6},{6,5},{7,8},{8,7},{9,10},{10,... | collective-permute-start | bytes 393224 | tf_op jit(solution)/shard_map/ppermute | solution.py:606
  55.2 12.5 %collective-permute-start.14 = (f32[16,512]{1,0:T(8,128)S(1)}, f32[16,512]{1,0:T(8,128)S(1)}, u32[]{:S(2)}, u32[]{:S(2)}) collective-permute-start(f32[16,512]{1,0:T(8,128)S(1)} %get-tuple-element.74), channel_id=1, source_target_pairs={{0,64},{64,0},{1,65},{65,1},{2,66},{66,2},{3,67},{67,3},{4,68},{68... | collective-permute-start | bytes 98312 | tf_op jit(solution)/shard_map/ppermute | solution.py:613
  59.2 5.4 %collective-permute-start.15 = (f32[16,128]{1,0:T(8,128)S(1)}, f32[16,128]{1,0:T(8,128)S(1)}, u32[]{:S(2)}, u32[]{:S(2)}) collective-permute-start(f32[16,128]{1,0:T(8,128)S(1)} %get-tuple-element.75), channel_id=1, source_target_pairs={{0,65},{1,64},{2,67},{3,66},{4,69},{5,68},{6,71},{7,70},{8,73},{9,... | collective-permute-start | bytes 24584 | tf_op jit(solution)/shard_map/ppermute | solution.py:610
  59.2 8.5 %collective-permute-start.16 = (f32[16,128]{1,0:T(8,128)S(1)}, f32[16,128]{1,0:T(8,128)S(1)}, u32[]{:S(2)}, u32[]{:S(2)}) collective-permute-start(f32[16,128]{1,0:T(8,128)S(1)} %get-tuple-element.76), channel_id=1, source_target_pairs={{0,127},{1,66},{2,65},{3,68},{4,67},{5,70},{6,69},{7,72},{8,71},{9... | collective-permute-start | bytes 24584 | tf_op jit(solution)/shard_map/ppermute | solution.py:610

commit v3 on v2

--- a/solution.py
+++ b/solution.py
@@ -260,14 +260,16 @@
     if have == width:
         return x
     side = (width - OWN) // 2
+    if side == 0:
+        return x[:, :OWN]
     return jnp.concatenate([x[:, : OWN + side], x[:, have - side :]], axis=1)
 
 
-def crit_step(cb, planes, v, near_u0, src, inv, wide=()):
+def crit_step(cb, planes, v, near_u0, src, inv, wide=(), bare=None):
     u = {d: mm(cb, x) for d, x in v.items()}
     out = {}
     for d in planes:
-        width = OWN + (4 if d in wide else 2) * T
+        width = OWN if d == bare else OWN + (4 if d in wide else 2) * T
         parts = []
         if d in u:
             masks = z_masks(u[d].shape[1])
@@ -281,7 +283,7 @@
         if src is not None:
             parts.append(src(d))
         c = functools.reduce(lambda a, b: a + b, [fit(x, width) for x in parts])
-        order = (0, 1, 2, -2, -1) if d in wide else (0, 1, -1)
+        order = (0,) if d == bare else (0, 1, 2, -2, -1) if d in wide else (0, 1, -1)
         pieces = []
         at = 0
         for i in order:
@@ -374,7 +376,7 @@
         near = mm(cb, jnp.concatenate([g[...], g_right, g_left], axis=1))[:S]
         for k in range(1, 5):
             vals = crit_step(
-                cb, range(5 - k), vals, near, lambda d: wide(src[d, :, :OWN], src[d, :, OWN:], sc, d), inv
+                cb, range(5 - k), vals, near, lambda d: wide(src[d, :, :OWN], src[d, :, OWN:], sc, d), inv, (), 4 - k
             )
         top = vals[0][:, :OWN]
         h[...] = top
@@ -524,7 +526,7 @@
             return jnp.concatenate([own, sc[0, :, :T], r, l, sc[0, :, T:]], axis=1)
 
         for k in range(3, 9):
-            vals = crit_step(cb, range(9 - k), vals, near, source, inv, (0,) if k == 3 else ())
+            vals = crit_step(cb, range(9 - k), vals, near, source, inv, (0,) if k == 3 else (), 8 - k)
         top = vals[0][:, :OWN]
         g8[...] = top
         put_edges(top, g8a, g8b, slice(None))

time: 73.6 us -> 73.6 us (level)
  no operation moved by 1% of the time
where the time goes in v3:
time: 73.6 us; the launch traced here: 73.5 us
  starting transfers between devices  30.3 us (41%)
  Pallas kernels  24.2 us (33%)
  waiting for transfers between devices  18.6 us (25%)
    ppermute x4, starting transfers between devices, swap_b(): return lax.ppermute(x, 'gy', list(enumerate(other)))  18.3 us
    pallas_call x4, Pallas kernels, call(): pl.pallas_call(kernel, in_specs=[vm] * len(ins), out_specs=[pl.BlockSpec(...  15.4 us
    ppermute x6, waiting for transfers between devices, cross(): return lax.ppermute(x, ('flow', 'gy'), pairs)  13.2 us
    ppermute x6, starting transfers between devices, cross(): return lax.ppermute(x, ('flow', 'gy'), pairs)  6.71 us
    pallas_call x1, Pallas kernels, pack(): pl.pallas_call(pack_kernel, in_specs=[hbm] * 3, out_specs=[hbm] * 4, out_...  4.84 us
    ppermute x3, starting transfers between devices, swap_f(): return lax.ppermute(x, 'flow', [(0, 1), (1, 0)])  4.83 us
    ppermute x4, waiting for transfers between devices, swap_b(): return lax.ppermute(x, 'gy', list(enumerate(other)))  4.27 us
    pallas_call x1, Pallas kernels, turn(): pl.pallas_call(turn_kernel, in_specs=[pl.BlockSpec(memory_space=pltpu.HBM...  3.99 us
  transfers between devices with their start and end apart: 17, of which 8 were waited for; matrix products, arithmetic and copies ran while one was open for 0% of the time, Pallas kernels for 12%

profile of v3, /device:TPU:0, one launch (start us, length us, event | category | flops | bytes accessed | tf_op | source)
XLA Modules:
  0.0 73.5 jit_solution(15951948164849745366)
XLA Ops:
  0.0 4.8 %pack.1 = (f32[1824,128]{1,0:T(8,128)}, f32[1824,128]{1,0:T(8,128)}, f32[1312,128]{1,0:T(8,128)}, f32[1312,128]{1,0:T(8,128)}) custom-call(f32[16,16,512]{2,1,0:T(8,128)} %state.3, f32[16,16,512]{2,1,0:T(8,128)} %src_in.1, f32[16,256,512]{2,1,0:T(8,128)} %bitcast.8), custom_call_target="tpu_custom_call" | custom-call | tf_op jit(solution)/shard_map/pack/pallas_call | solution.py:185
  4.9 9.1 %collective-permute-start.4 = (f32[1824,128]{1,0:T(8,128)}, f32[1824,128]{1,0:T(8,128)S(1)}, u32[]{:S(2)}, u32[]{:S(2)}) collective-permute-start(f32[1824,128]{1,0:T(8,128)} %get-tuple-element.46), channel_id=1, source_target_pairs={{0,63},{1,2},{2,1},{3,4},{4,3},{5,6},{6,5},{7,8},{8,7},{9,10},{10,... | collective-permute-start | bytes 2801672 | tf_op jit(solution)/shard_map/ppermute | solution.py:608
  14.1 0.7 collective-permute-start.1
  14.8 0.1 collective-permute-start.2
  14.9 4.0 %turn.1.own_inv = f32[16,16,16,512]{3,2,1,0:T(8,128)S(1)} custom-call(f32[16,256,512]{2,1,0:T(8,128)} %bitcast.9), custom_call_target="tpu_custom_call" | custom-call | tf_op jit(solution)/shard_map/turn/pallas_call | solution.py:225
  18.9 5.2 %collective-permute-done.3.gb = f32[16,128]{1,0:T(8,128)S(1)} collective-permute-done((f32[16,128]{1,0:T(8,128)S(1)}, f32[16,128]{1,0:T(8,128)S(1)}, u32[]{:S(2)}, u32[]{:S(2)}) %collective-permute-start.3) | collective-permute-done | bytes 8224 | tf_op jit(solution)/shard_map/ppermute | solution.py:612
  24.1 1.8 %collective-permute-done.2.ga = f32[16,128]{1,0:T(8,128)S(1)} collective-permute-done((f32[16,128]{1,0:T(8,128)S(1)}, f32[16,128]{1,0:T(8,128)S(1)}, u32[]{:S(2)}, u32[]{:S(2)}) %collective-permute-start.2) | collective-permute-done | bytes 8224 | tf_op jit(solution)/shard_map/ppermute | solution.py:612
  25.9 1.0 %collective-permute-done.1.g = f32[16,512]{1,0:T(8,128)S(1)} collective-permute-done((f32[16,512]{1,0:T(8,128)S(1)}, f32[16,512]{1,0:T(8,128)S(1)}, u32[]{:S(2)}, u32[]{:S(2)}) %collective-permute-start.1) | collective-permute-done | bytes 32800 | tf_op jit(solution)/shard_map/ppermute | solution.py:615
  26.9 0.2 collective-permute-start.5
  27.1 0.9 %collective-permute-start.11 = (f32[1312,128]{1,0:T(8,128)S(1)}, f32[1312,128]{1,0:T(8,128)S(1)}, u32[]{:S(2)}, u32[]{:S(2)}) collective-permute-start(f32[1312,128]{1,0:T(8,128)S(1)} %copy-done.3), channel_id=1, source_target_pairs={{0,63},{1,2},{2,1},{3,4},{4,3},{5,6},{6,5},{7,8},{8,7},{9,10},{10,... | collective-permute-start | bytes 2015240 | tf_op jit(solution)/shard_map/ppermute | solution.py:608
  28.0 4.8 %first.1 = (f32[16,16,512]{2,1,0:T(8,128)S(1)}, f32[18,16,128]{2,1,0:T(8,128)S(1)}, f32[18,16,128]{2,1,0:T(8,128)S(1)}, f32[16,512]{1,0:T(8,128)S(1)}, f32[16,25...) custom-call(f32[48,16]{1,0:T(8,128)S(1)} %bitcast.4, ...), custom_call_target="tpu_custom_call" | custom-call | tf_op jit(solution)/shard_map/first/pallas_call | solution.py:583
  32.8 6.7 %collective-permute-start.7 = (f32[18,16,128]{2,1,0:T(8,128)S(1)}, f32[18,16,128]{2,1,0:T(8,128)S(1)}, u32[]{:S(2)}, u32[]{:S(2)}) collective-permute-start(f32[18,16,128]{2,1,0:T(8,128)S(1)} %get-tuple-element.60), channel_id=1, source_target_pairs={{0,63},{1,2},{2,1},{3,4},{4,3},{5,6},{6,5},{7,8},{8,7},{9,10},{10,... | collective-permute-start | bytes 442376 | tf_op jit(solution)/shard_map/ppermute | solution.py:608
  39.5 0.1 collective-permute-start.8
  39.7 1.2 %collective-permute-start.10 = (f32[16,256]{1,0:T(8,128)S(1)}, f32[16,256]{1,0:T(8,128)S(1)}, u32[]{:S(2)}, u32[]{:S(2)}) collective-permute-start(f32[16,256]{1,0:T(8,128)S(1)} %get-tuple-element.66), channel_id=1, source_target_pairs={{0,127},{1,66},{2,65},{3,68},{4,67},{5,70},{6,69},{7,72},{8,71},{9... | collective-permute-start | bytes 49160 | tf_op jit(solution)/shard_map/ppermute | solution.py:612
  40.9 2.5 %collective-permute-done.11.pb2 = f32[1312,128]{1,0:T(8,128)S(1)} collective-permute-done((f32[1312,128]{1,0:T(8,128)S(1)}, f32[1312,128]{1,0:T(8,128)S(1)}, u32[]{:S(2)}, u32[]{:S(2)}) %collective-permute-start.11) | collective-permute-done | bytes 671776 | tf_op jit(solution)/shard_map/ppermute | solution.py:608
  43.3 0.1 collective-permute-done.8.h
  43.5 1.8 %collective-permute-done.7.eb_in = f32[18,16,128]{2,1,0:T(8,128)S(1)} collective-permute-done((f32[18,16,128]{2,1,0:T(8,128)S(1)}, f32[18,16,128]{2,1,0:T(8,128)S(1)}, u32[]{:S(2)}, u32[]{:S(2)}) %collective-permute-start.7) | collective-permute-done | bytes 147488 | tf_op jit(solution)/shard_map/ppermute | solution.py:608
  45.3 3.1 %collective-permute-done.10.hb = f32[16,256]{1,0:T(8,128)S(1)} collective-permute-done((f32[16,256]{1,0:T(8,128)S(1)}, f32[16,256]{1,0:T(8,128)S(1)}, u32[]{:S(2)}, u32[]{:S(2)}) %collective-permute-start.10) | collective-permute-done | bytes 16416 | tf_op jit(solution)/shard_map/ppermute | solution.py:612
  48.4 4.9 %second.1 = (f32[16,16,512]{2,1,0:T(8,128)S(1)}, f32[16,16,128]{2,1,0:T(8,128)S(1)}, f32[16,16,128]{2,1,0:T(8,128)S(1)}, f32[16,16,16,128]{3,2,1,0:T(8,128)S(1)}) custom-call(f32[48,16]{1,0:T(8,128)S(1)} %bitcast.5, f32[16,16,512]{2,1,0:T(8,128)S(1)} %get-tuple-element.50.v_in, f32[18,16,128]{2,1,0:T(8,128)S(1)} %collective-permute-done.6.ea_in, ...), custom_call_target="tpu_custom_call" | custom-call | tf_op jit(solution)/shard_map/second/pallas_call | solution.py:583
  53.4 1.7 %collective-permute-start.13 = (f32[16,16,128]{2,1,0:T(8,128)S(1)}, f32[16,16,128]{2,1,0:T(8,128)S(1)}, u32[]{:S(2)}, u32[]{:S(2)}) collective-permute-start(f32[16,16,128]{2,1,0:T(8,128)S(1)} %get-tuple-element.71), channel_id=1, source_target_pairs={{0,63},{1,2},{2,1},{3,4},{4,3},{5,6},{6,5},{7,8},{8,7},{9,10},{10,... | collective-permute-start | bytes 393224 | tf_op jit(solution)/shard_map/ppermute | solution.py:608
  55.2 4.0 %collective-permute-start.14 = (f32[16,512]{1,0:T(8,128)S(1)}, f32[16,512]{1,0:T(8,128)S(1)}, u32[]{:S(2)}, u32[]{:S(2)}) collective-permute-start(f32[16,512]{1,0:T(8,128)S(1)} %get-tuple-element.74), channel_id=1, source_target_pairs={{0,64},{64,0},{1,65},{65,1},{2,66},{66,2},{3,67},{67,3},{4,68},{68... | collective-permute-start | bytes 98312 | tf_op jit(solution)/shard_map/ppermute | solution.py:615
  59.2 5.4 %collective-permute-start.16 = (f32[16,128]{1,0:T(8,128)S(1)}, f32[16,128]{1,0:T(8,128)S(1)}, u32[]{:S(2)}, u32[]{:S(2)}) collective-permute-start(f32[16,128]{1,0:T(8,128)S(1)} %get-tuple-element.76), channel_id=1, source_target_pairs={{0,127},{1,66},{2,65},{3,68},{4,67},{5,70},{6,69},{7,72},{8,71},{9... | collective-permute-start | bytes 24584 | tf_op jit(solution)/shard_map/ppermute | solution.py:612
  64.6 3.1 %collective-permute-done.16.g8b = f32[16,128]{1,0:T(8,128)S(1)} collective-permute-done((f32[16,128]{1,0:T(8,128)S(1)}, f32[16,128]{1,0:T(8,128)S(1)}, u32[]{:S(2)}, u32[]{:S(2)}) %collective-permute-start.16) | collective-permute-done | bytes 8224 | tf_op jit(solution)/shard_map/ppermute | solution.py:612
  67.7 5.6 %third.1 = f32[16,16,512]{2,1,0:T(8,128)} custom-call(f32[48,16]{1,0:T(8,128)S(1)} %bitcast.7, f32[16,16,512]{2,1,0:T(8,128)S(1)} %get-tuple-element.69.v_in, f32[16,16,128]{2,1,0:T(8,128)S(1)} %collective-permute-done.12.ea_in, f32[16,16,128]{2,1,0:T(8,128)S(1)} %collective-permute-done.13.eb_in, f32[16,16,16,512]{3,2,1,0:T(8,128)S(1)} %turn.1.own_inv, ...), custom_call_target="tpu_custom_call" | custom-call | tf_op jit(solution)/shard_map/third/pallas_call | solution.py:583
  (28 shorter events, 0.4 us)
Async XLA Ops:
  0.0 14.1 %copy-start = (f32[16,16,512]{2,1,0:T(8,128)S(1)}, f32[16,16,512]{2,1,0:T(8,128)}, u32[]{:S(2)}) copy-start(f32[16,16,512]{2,1,0:T(8,128)} %state.3) | copy-start | bytes 1572868
  4.9 22.0 %collective-permute-start = (f32[1824,128]{1,0:T(8,128)}, f32[1824,128]{1,0:T(8,128)S(1)}, u32[]{:S(2)}, u32[]{:S(2)}) collective-permute-start(f32[1824,128]{1,0:T(8,128)} %get-tuple-element.41), channel_id=1, source_target_pairs={{0,1},{1,0},{2,3},{3,2},{4,5},{5,4},{6,7},{7,6},{8,9},{9,8},{10,11... | collective-permute-start | bytes 2801672 | tf_op jit(solution)/shard_map/ppermute | solution.py:605
  4.9 23.0 %collective-permute-start.4 = (f32[1824,128]{1,0:T(8,128)}, f32[1824,128]{1,0:T(8,128)S(1)}, u32[]{:S(2)}, u32[]{:S(2)}) collective-permute-start(f32[1824,128]{1,0:T(8,128)} %get-tuple-element.46), channel_id=1, source_target_pairs={{0,63},{1,2},{2,1},{3,4},{4,3},{5,6},{6,5},{7,8},{8,7},{9,10},{10,... | collective-permute-start | bytes 2801672 | tf_op jit(solution)/shard_map/ppermute | solution.py:608
  14.1 12.8 %collective-permute-start.1 = (f32[16,512]{1,0:T(8,128)S(1)}, f32[16,512]{1,0:T(8,128)S(1)}, u32[]{:S(2)}, u32[]{:S(2)}) collective-permute-start(f32[16,512]{1,0:T(8,128)S(1)} %select_bitcast_fusion), channel_id=1, source_target_pairs={{0,64},{64,0},{1,65},{65,1},{2,66},{66,2},{3,67},{67,3},{4,68},{68... | collective-permute-start | bytes 98312 | tf_op jit(solution)/shard_map/ppermute | solution.py:615
  14.8 9.3 %collective-permute-start.3 = (f32[16,128]{1,0:T(8,128)S(1)}, f32[16,128]{1,0:T(8,128)S(1)}, u32[]{:S(2)}, u32[]{:S(2)}) collective-permute-start(f32[16,128]{1,0:T(8,128)S(1)} %get-tuple-element.77), channel_id=1, source_target_pairs={{0,127},{1,66},{2,65},{3,68},{4,67},{5,70},{6,69},{7,72},{8,71},{9... | collective-permute-start | bytes 24584 | tf_op jit(solution)/shard_map/ppermute | solution.py:612
  14.8 12.1 %copy-start.4 = (f32[1312,128]{1,0:T(8,128)S(1)}, f32[1312,128]{1,0:T(8,128)}, u32[]{:S(2)}) copy-start(f32[1312,128]{1,0:T(8,128)} %get-tuple-element.56) | copy-start | bytes 2015236
  14.8 12.3 %copy-start.3 = (f32[1312,128]{1,0:T(8,128)S(1)}, f32[1312,128]{1,0:T(8,128)}, u32[]{:S(2)}) copy-start(f32[1312,128]{1,0:T(8,128)} %get-tuple-element.68) | copy-start | bytes 2015236
  14.8 13.2 %copy-start.1 = (f32[16,16,512]{2,1,0:T(8,128)S(1)}, f32[16,16,512]{2,1,0:T(8,128)}, u32[]{:S(2)}) copy-start(f32[16,16,512]{2,1,0:T(8,128)} %src_in.1) | copy-start | bytes 1572868
  14.8 13.2 %copy-start.2 = (f32[3,16,16]{2,1,0:T(8,128)S(1)}, f32[3,16,16]{2,1,0:T(8,128)}, u32[]{:S(2)}) copy-start(f32[3,16,16]{2,1,0:T(8,128)} %param.7) | copy-start | bytes 9220
  14.8 11.1 %collective-permute-start.2 = (f32[16,128]{1,0:T(8,128)S(1)}, f32[16,128]{1,0:T(8,128)S(1)}, u32[]{:S(2)}, u32[]{:S(2)}) collective-permute-start(f32[16,128]{1,0:T(8,128)S(1)} %get-tuple-element.78), channel_id=1, source_target_pairs={{0,65},{1,64},{2,67},{3,66},{4,69},{5,68},{6,71},{7,70},{8,73},{9,... | collective-permute-start | bytes 24584 | tf_op jit(solution)/shard_map/ppermute | solution.py:612
  26.9 5.9 %collective-permute-start.5 = (f32[1312,128]{1,0:T(8,128)S(1)}, f32[1312,128]{1,0:T(8,128)S(1)}, u32[]{:S(2)}, u32[]{:S(2)}) collective-permute-start(f32[1312,128]{1,0:T(8,128)S(1)} %copy-done.4), channel_id=1, source_target_pairs={{0,1},{1,0},{2,3},{3,2},{4,5},{5,4},{6,7},{7,6},{8,9},{9,8},{10,11... | collective-permute-start | bytes 2015240 | tf_op jit(solution)/shard_map/ppermute | solution.py:605
  27.1 16.3 %collective-permute-start.11 = (f32[1312,128]{1,0:T(8,128)S(1)}, f32[1312,128]{1,0:T(8,128)S(1)}, u32[]{:S(2)}, u32[]{:S(2)}) collective-permute-start(f32[1312,128]{1,0:T(8,128)S(1)} %copy-done.3), channel_id=1, source_target_pairs={{0,63},{1,2},{2,1},{3,4},{4,3},{5,6},{6,5},{7,8},{8,7},{9,10},{10,... | collective-permute-start | bytes 2015240 | tf_op jit(solution)/shard_map/ppermute | solution.py:608
  32.7 6.9 %collective-permute-start.6 = (f32[18,16,128]{2,1,0:T(8,128)S(1)}, f32[18,16,128]{2,1,0:T(8,128)S(1)}, u32[]{:S(2)}, u32[]{:S(2)}) collective-permute-start(f32[18,16,128]{2,1,0:T(8,128)S(1)} %get-tuple-element.57), channel_id=1, source_target_pairs={{0,1},{1,0},{2,3},{3,2},{4,5},{5,4},{6,7},{7,6},{8,9},{9,8},{10,11... | collective-permute-start | bytes 442376 | tf_op jit(solution)/shard_map/ppermute | solution.py:605
  32.8 12.4 %collective-permute-start.7 = (f32[18,16,128]{2,1,0:T(8,128)S(1)}, f32[18,16,128]{2,1,0:T(8,128)S(1)}, u32[]{:S(2)}, u32[]{:S(2)}) collective-permute-start(f32[18,16,128]{2,1,0:T(8,128)S(1)} %get-tuple-element.60), channel_id=1, source_target_pairs={{0,63},{1,2},{2,1},{3,4},{4,3},{5,6},{6,5},{7,8},{8,7},{9,10},{10,... | collective-permute-start | bytes 442376 | tf_op jit(solution)/shard_map/ppermute | solution.py:608
  39.5 4.0 %collective-permute-start.8 = (f32[16,512]{1,0:T(8,128)S(1)}, f32[16,512]{1,0:T(8,128)S(1)}, u32[]{:S(2)}, u32[]{:S(2)}) collective-permute-start(f32[16,512]{1,0:T(8,128)S(1)} %get-tuple-element.64), channel_id=1, source_target_pairs={{0,64},{64,0},{1,65},{65,1},{2,66},{66,2},{3,67},{67,3},{4,68},{68... | collective-permute-start | bytes 98312 | tf_op jit(solution)/shard_map/ppermute | solution.py:615
  39.7 3.7 %collective-permute-start.9 = (f32[16,256]{1,0:T(8,128)S(1)}, f32[16,256]{1,0:T(8,128)S(1)}, u32[]{:S(2)}, u32[]{:S(2)}) collective-permute-start(f32[16,256]{1,0:T(8,128)S(1)} %get-tuple-element.65), channel_id=1, source_target_pairs={{0,65},{1,64},{2,67},{3,66},{4,69},{5,68},{6,71},{7,70},{8,73},{9,... | collective-permute-start | bytes 49160 | tf_op jit(solution)/shard_map/ppermute | solution.py:612
  39.7 8.7 %collective-permute-start.10 = (f32[16,256]{1,0:T(8,128)S(1)}, f32[16,256]{1,0:T(8,128)S(1)}, u32[]{:S(2)}, u32[]{:S(2)}) collective-permute-start(f32[16,256]{1,0:T(8,128)S(1)} %get-tuple-element.66), channel_id=1, source_target_pairs={{0,127},{1,66},{2,65},{3,68},{4,67},{5,70},{6,69},{7,72},{8,71},{9... | collective-permute-start | bytes 49160 | tf_op jit(solution)/shard_map/ppermute | solution.py:612
  53.3 14.4 %collective-permute-start.12 = (f32[16,16,128]{2,1,0:T(8,128)S(1)}, f32[16,16,128]{2,1,0:T(8,128)S(1)}, u32[]{:S(2)}, u32[]{:S(2)}) collective-permute-start(f32[16,16,128]{2,1,0:T(8,128)S(1)} %get-tuple-element.70), channel_id=1, source_target_pairs={{0,1},{1,0},{2,3},{3,2},{4,5},{5,4},{6,7},{7,6},{8,9},{9,8},{10,11... | collective-permute-start | bytes 393224 | tf_op jit(solution)/shard_map/ppermute | solution.py:605
  53.4 14.3 %collective-permute-start.13 = (f32[16,16,128]{2,1,0:T(8,128)S(1)}, f32[16,16,128]{2,1,0:T(8,128)S(1)}, u32[]{:S(2)}, u32[]{:S(2)}) collective-permute-start(f32[16,16,128]{2,1,0:T(8,128)S(1)} %get-tuple-element.71), channel_id=1, source_target_pairs={{0,63},{1,2},{2,1},{3,4},{4,3},{5,6},{6,5},{7,8},{8,7},{9,10},{10,... | collective-permute-start | bytes 393224 | tf_op jit(solution)/shard_map/ppermute | solution.py:608
  55.2 12.5 %collective-permute-start.14 = (f32[16,512]{1,0:T(8,128)S(1)}, f32[16,512]{1,0:T(8,128)S(1)}, u32[]{:S(2)}, u32[]{:S(2)}) collective-permute-start(f32[16,512]{1,0:T(8,128)S(1)} %get-tuple-element.74), channel_id=1, source_target_pairs={{0,64},{64,0},{1,65},{65,1},{2,66},{66,2},{3,67},{67,3},{4,68},{68... | collective-permute-start | bytes 98312 | tf_op jit(solution)/shard_map/ppermute | solution.py:615
  59.2 5.4 %collective-permute-start.15 = (f32[16,128]{1,0:T(8,128)S(1)}, f32[16,128]{1,0:T(8,128)S(1)}, u32[]{:S(2)}, u32[]{:S(2)}) collective-permute-start(f32[16,128]{1,0:T(8,128)S(1)} %get-tuple-element.75), channel_id=1, source_target_pairs={{0,65},{1,64},{2,67},{3,66},{4,69},{5,68},{6,71},{7,70},{8,73},{9,... | collective-permute-start | bytes 24584 | tf_op jit(solution)/shard_map/ppermute | solution.py:612
  59.2 8.5 %collective-permute-start.16 = (f32[16,128]{1,0:T(8,128)S(1)}, f32[16,128]{1,0:T(8,128)S(1)}, u32[]{:S(2)}, u32[]{:S(2)}) collective-permute-start(f32[16,128]{1,0:T(8,128)S(1)} %get-tuple-element.76), channel_id=1, source_target_pairs={{0,127},{1,66},{2,65},{3,68},{4,67},{5,70},{6,69},{7,72},{8,71},{9... | collective-permute-start | bytes 24584 | tf_op jit(solution)/shard_map/ppermute | solution.py:612
